TPU v7x, 256 devices: a whole 4x4x8 slice. The times are simulated.
256 devices in a mesh: section: 2 (over y_hi), seq: 32 (over y_lo, z, core), tensor: 4 (over x).
Axes of the slice: x: 4, y: 4 (y_hi: 2, y_lo: 2; y = y_hi * 2 + y_lo), z: 8, core: 2. Of those that a mesh axis runs over, the one named last changes fastest.
Arguments:
- token_ids: int32 [2, 4352], P(None, 'seq'), may hold values from 0 to 511
- embed_table: bfloat16 [512, 4096], P(None, 'tensor')
- norm_gain: float32 [2, 4096], P('section'), may hold values from 0.1 to 1.9
- in_weight: bfloat16 [2, 4096, 3, 4096], P('section', 'seq', None, 'tensor'), may hold values from -0.09375 to 0.09375
- se_filter: float32 [2, 3, 7, 4096], P('section', None, None, 'tensor'), may hold values from -2.4 to 2.4
- mr_filter: float32 [2, 128, 4096], P('section', None, 'tensor'), may hold values from -0.54 to 0.54
- out_weight: bfloat16 [2, 4096, 4096], P('section', 'tensor')
Outputs:
- section_out: bfloat16 [2, 2, 4352, 4096], P('section', None, 'seq', 'tensor')
All inputs are finite; a program needn't handle non-finite values.
Results may differ from a plain program's by a relative error of at most 0.025.
Values may be sent and summed in bfloat16 or wider, within the bound.
A program may use at most 192 MiB of HBM per device.

v0:
```python
import jax
import jax.numpy as jnp
from jax import lax
from jax.sharding import PartitionSpec as P

EPS = 1e-06


def passed_along(value, axis, steps):
    count = lax.axis_size(axis)
    initial, last = (max(0, -steps), min(count, count - steps))
    return lax.ppermute(value, axis, [(source, source + steps) for source in range(initial, last)])


def causal_sum(extended, coeffs, length):
    taps = coeffs.shape[0]
    total = jnp.zeros((length,) + extended.shape[1:], jnp.float32)
    for tap in range(taps):
        begin = taps - 1 - tap
        total = total + coeffs[tap][None] * extended[begin : begin + length]
    return total


def body(token_ids, embed_table, norm_gain, in_weight, se_filter, mr_filter, out_weight):
    micro = token_ids.shape[0]
    length = token_ids.shape[1]
    vocab = embed_table.shape[0]
    width = embed_table.shape[1]
    full_width = width * lax.axis_size("tensor")
    sections = lax.axis_size("section")
    section = lax.axis_index("section")
    gain_full = norm_gain[0]
    gain_local = lax.dynamic_slice_in_dim(gain_full, lax.axis_index("tensor") * width, width, 0)
    short_coeffs = jnp.transpose(se_filter[0], (1, 0, 2))
    medium_taps = mr_filter[0]
    weight = out_weight[0]
    se_count = short_coeffs.shape[0]
    mr_count = medium_taps.shape[0]
    in_full = lax.all_gather(in_weight[0], "seq", axis=0, tiled=True).reshape(full_width, 3 * width)

    def project_in(piece):
        return jnp.dot(piece, in_full, preferred_element_type=jnp.float32)

    def section_layer(stream):
        values = stream.astype(jnp.float32)
        squares = lax.psum(jnp.sum(values * values, axis=1), "tensor")
        scale = lax.rsqrt(squares / full_width + EPS)
        normed = (values * scale[:, None] * gain_local[None, :]).astype(jnp.bfloat16)
        proj_sum = project_in(lax.all_gather(normed, "tensor", axis=1, tiled=True))
        streams = proj_sum.astype(jnp.bfloat16).reshape(length, 3, width)
        rim = passed_along(streams[length - (se_count - 1) :], "seq", 1)
        reach = jnp.concatenate([rim, streams], axis=0).astype(jnp.float32)
        short = causal_sum(reach, short_coeffs, length)
        gated = (short[:, 1] * short[:, 2]).astype(jnp.bfloat16)
        query = short[:, 0]
        second_rim = passed_along(gated[length - (mr_count - 1) :], "seq", 1)
        gated_ext = jnp.concatenate([second_rim, gated], axis=0)
        medium = causal_sum(gated_ext.astype(jnp.float32), medium_taps, length)
        mixed = (query * medium).astype(jnp.bfloat16)
        partial_terms = jnp.dot(mixed, weight, preferred_element_type=jnp.float32)
        projected = lax.psum_scatter(
            partial_terms.astype(jnp.bfloat16), "tensor", scatter_dimension=1, tiled=True
        ).astype(jnp.float32)
        return (values + projected).astype(jnp.bfloat16)

    vocab_index = jnp.arange(vocab, dtype=jnp.int32)

    def one_turn(turn, carry):
        arrived, results = carry
        offset = turn - section
        slot = jnp.clip(offset, 0, micro - 1)
        ids = lax.dynamic_index_in_dim(token_ids, slot, 0, keepdims=False)
        onehot = (ids[:, None] == vocab_index[None, :]).astype(jnp.bfloat16)
        embedded = jnp.dot(onehot, embed_table, preferred_element_type=jnp.float32).astype(
            jnp.bfloat16
        )
        stream = jnp.where(section == 0, embedded, arrived)
        produced = section_layer(stream)
        valid = jnp.logical_and(offset >= 0, offset < micro)
        previous = lax.dynamic_index_in_dim(results, slot, 0, keepdims=False)
        results = lax.dynamic_update_index_in_dim(
            results, jnp.where(valid, produced, previous), slot, 0
        )
        arrived = passed_along(produced, "section", 1)
        return (arrived, results)

    start_stream = jnp.zeros((length, width), jnp.bfloat16)
    start_results = jnp.zeros((micro, length, width), jnp.bfloat16)
    arrived, results = lax.fori_loop(
        0, micro + sections - 1, one_turn, (start_stream, start_results)
    )
    return results[None]


def solution(mesh):
    in_specs = (
        P(None, "seq"),
        P(None, "tensor"),
        P("section", None),
        P("section", "seq", None, "tensor"),
        P("section", None, None, "tensor"),
        P("section", None, "tensor"),
        P("section", "tensor", None),
    )
    out_specs = P("section", None, "seq", "tensor")
    return jax.shard_map(body, mesh=mesh, in_specs=in_specs, out_specs=out_specs, check_vma=False)
```

profile of v0, /device:TPU:26, one launch (start us, length us, event | category | flops | bytes accessed | tf_op | source)
XLA Modules:
  0.0 601.0 jit_solution(5382177293395175838)
XLA Ops:
  6.5 2.3 copy.16
  9.0 165.6 %all-gather.4.cloned.1.call-done = bf16[1,4096,3,1024]{1,3,2,0:T(8,128)(2,1)} async-done(((bf16[1,128,3,1024]{1,3,2,0:T(8,128)(2,1)}), bf16[1,4096,3,1024]{1,3,2,0:T(8,128)(2,1)}) %all-gather.4.cloned.1.call-update) | async-done | bytes 25165840 | tf_op jit(solution)/shard_map/all_gather | solution.py:39
  174.6 32.7 %copy.17 = bf16[4096,3072]{1,0:T(8,128)(2,1)} copy(bf16[4096,3072]{0,1:T(8,128)(2,1)} %bitcast.451) | data formatting | bytes 50331648
  208.2 385.3 %while.17 = (s32[]{:T(128)}, bf16[136,1024]{1,0:T(8,128)(2,1)S(1)}, bf16[2,136,1024]{2,1,0:T(8,128)(2,1)}, pred[]{:T(512)}, s32[]{:T(128)}, /*index=5*/s32[2,136...) while((s32[]{:T(128)}, bf16[136,1024]{1,0:T(8,128)(2,1)S(1)}, ...), condition=%wide.region_4.5_spmd.clone, body=%wide.region_0.4_spmd.clone.sunk | while | flops 4752175104 | bytes 154546512 | solution.py:89
  208.9 1.7 multiply_reduce_fusion.2
  210.6 8.6 %psum.14 = f32[136]{0:T(256)S(1)} all-reduce(f32[136]{0:T(256)S(1)} %get-tuple-element.688), channel_id=1, replica_groups=mesh['section'=2,'seq'=32,'tensor'=4] {'tensor'}, use_global_device_ids=true, to_apply=%region_2.2 | all-reduce | flops 136 | bytes 1088 | tf_op jit(solution)/shard_map/while/body/eval_jaxpr/psum | solution.py:46
  222.3 22.4 %all-gather.6.cloned.1.call-done = bf16[136,4096]{1,0:T(8,128)(2,1)} async-done(((bf16[136,1024]{1,0:T(8,128)(2,1)}), bf16[136,4096]{1,0:T(8,128)(2,1)}) %all-gather.6.cloned.1.call-update) | async-done | bytes 1114128 | tf_op jit(solution)/shard_map/while/body/eval_jaxpr/all_gather | solution.py:49
  244.7 12.1 %convolution_convert_fusion.5 = bf16[136,3072]{1,0:T(8,128)(2,1)S(1)} fusion(bf16[136,4096]{1,0:T(8,128)(2,1)} %all-gather.6.cloned.1.call-done, bf16[4096,3072]{1,0:T(8,128)(2,1)} %get-tuple-element.867), kind=kOutput, calls=%fused_computation.2.clone.1 | convolution fusion | flops 3422969856 | bytes 27115520 | tf_op jit(solution)/shard_map/while/body/eval_jaxpr/dot_general | solution.py:42
  256.9 1.9 collective-permute-start
  259.5 1.2 reshape.29
  260.7 3.7 collective-permute-done
  265.1 4.2 fusion.174
  269.3 1.1 fusion.175
  271.4 1.9 collective-permute-start.1
  273.6 7.7 %collective-permute-done.1 = bf16[127,1024]{1,0:T(8,128)(2,1)S(1)} collective-permute-done((bf16[127,1024]{1,0:T(8,128)(2,1)S(1)}, bf16[127,1024]{1,0:T(8,128)(2,1)S(1)}, u32[]{:S(2)}, u32[]{:S(2)}) %collective-permute-start.1) | collective-permute-done | bytes 260128 | tf_op jit(solution)/shard_map/while/body/eval_jaxpr/ppermute | solution.py:12
  281.8 16.9 %convolution_convert_fusion.6 = bf16[136,4096]{1,0:T(8,128)(2,1)} fusion(bf16[1024,4096]{1,0:T(8,128)(2,1)} %get-tuple-element.869, f32[263,1024]{1,0:T(8,128)S(1)} %maximum_convert_fusion.5, f32[1024]{0:T(1024)S(1)} %bitcast.458, f32[1024]{0:T(1024)S(1)} %bitcast.459, f32[1024]{0:T(1024)S(1)} %bitcast.460, f32[1024]{0:T(1024)S(1)} %bitcast.461, ...), kind=kOutput, calls=%fused_computation.1.clone.1 | convolution fusion | flops 1177198592 | bytes 81887232 | tf_op jit(solution)/shard_map/while/body/eval_jaxpr/dot_general | solution.py:60
  298.8 24.3 %reduce-scatter.2.cloned.1.call-done = bf16[136,1024]{1,0:T(8,128)(2,1)} async-done(((bf16[136,4096]{1,0:T(8,128)(2,1)}), bf16[136,1024]{1,0:T(8,128)(2,1)}) %reduce-scatter.2.cloned.1.call-update) | async-done | bytes 278544 | tf_op jit(solution)/shard_map/while/body/eval_jaxpr/reduce_scatter | solution.py:61
  324.2 1.3 collective-permute-start.2
  325.5 9.5 %collective-permute-done.2 = bf16[136,1024]{1,0:T(8,128)(2,1)S(1)} collective-permute-done((bf16[136,1024]{1,0:T(8,128)(2,1)S(1)}, bf16[136,1024]{1,0:T(8,128)(2,1)S(1)}, u32[]{:S(2)}, u32[]{:S(2)}) %collective-permute-start.2) | collective-permute-done | bytes 278560 | tf_op jit(solution)/shard_map/while/body/eval_jaxpr/ppermute | solution.py:12
  335.7 1.7 multiply_reduce_fusion.2
  337.4 10.0 %psum.14 = f32[136]{0:T(256)S(1)} all-reduce(f32[136]{0:T(256)S(1)} %get-tuple-element.688), channel_id=1, replica_groups=mesh['section'=2,'seq'=32,'tensor'=4] {'tensor'}, use_global_device_ids=true, to_apply=%region_2.2 | all-reduce | flops 136 | bytes 1088 | tf_op jit(solution)/shard_map/while/body/eval_jaxpr/psum | solution.py:46
  350.5 23.4 %all-gather.6.cloned.1.call-done = bf16[136,4096]{1,0:T(8,128)(2,1)} async-done(((bf16[136,1024]{1,0:T(8,128)(2,1)}), bf16[136,4096]{1,0:T(8,128)(2,1)}) %all-gather.6.cloned.1.call-update) | async-done | bytes 1114128 | tf_op jit(solution)/shard_map/while/body/eval_jaxpr/all_gather | solution.py:49
  373.9 12.1 %convolution_convert_fusion.5 = bf16[136,3072]{1,0:T(8,128)(2,1)S(1)} fusion(bf16[136,4096]{1,0:T(8,128)(2,1)} %all-gather.6.cloned.1.call-done, bf16[4096,3072]{1,0:T(8,128)(2,1)} %get-tuple-element.867), kind=kOutput, calls=%fused_computation.2.clone.1 | convolution fusion | flops 3422969856 | bytes 27115520 | tf_op jit(solution)/shard_map/while/body/eval_jaxpr/dot_general | solution.py:42
  386.2 1.9 collective-permute-start
  388.8 1.2 reshape.29
  390.0 3.7 collective-permute-done
  394.4 4.2 fusion.174
  398.5 1.1 fusion.175
  400.7 1.9 collective-permute-start.1
  402.8 7.7 %collective-permute-done.1 = bf16[127,1024]{1,0:T(8,128)(2,1)S(1)} collective-permute-done((bf16[127,1024]{1,0:T(8,128)(2,1)S(1)}, bf16[127,1024]{1,0:T(8,128)(2,1)S(1)}, u32[]{:S(2)}, u32[]{:S(2)}) %collective-permute-start.1) | collective-permute-done | bytes 260128 | tf_op jit(solution)/shard_map/while/body/eval_jaxpr/ppermute | solution.py:12
  411.0 16.9 %convolution_convert_fusion.6 = bf16[136,4096]{1,0:T(8,128)(2,1)} fusion(bf16[1024,4096]{1,0:T(8,128)(2,1)} %get-tuple-element.869, f32[263,1024]{1,0:T(8,128)S(1)} %maximum_convert_fusion.5, f32[1024]{0:T(1024)S(1)} %bitcast.458, f32[1024]{0:T(1024)S(1)} %bitcast.459, f32[1024]{0:T(1024)S(1)} %bitcast.460, f32[1024]{0:T(1024)S(1)} %bitcast.461, ...), kind=kOutput, calls=%fused_computation.1.clone.1 | convolution fusion | flops 1177198592 | bytes 81887232 | tf_op jit(solution)/shard_map/while/body/eval_jaxpr/dot_general | solution.py:60
  428.0 24.3 %reduce-scatter.2.cloned.1.call-done = bf16[136,1024]{1,0:T(8,128)(2,1)} async-done(((bf16[136,4096]{1,0:T(8,128)(2,1)}), bf16[136,1024]{1,0:T(8,128)(2,1)}) %reduce-scatter.2.cloned.1.call-update) | async-done | bytes 278544 | tf_op jit(solution)/shard_map/while/body/eval_jaxpr/reduce_scatter | solution.py:61
  453.4 1.3 collective-permute-start.2
  454.7 9.6 %collective-permute-done.2 = bf16[136,1024]{1,0:T(8,128)(2,1)S(1)} collective-permute-done((bf16[136,1024]{1,0:T(8,128)(2,1)S(1)}, bf16[136,1024]{1,0:T(8,128)(2,1)S(1)}, u32[]{:S(2)}, u32[]{:S(2)}) %collective-permute-start.2) | collective-permute-done | bytes 278560 | tf_op jit(solution)/shard_map/while/body/eval_jaxpr/ppermute | solution.py:12
  465.0 1.7 multiply_reduce_fusion.2
  466.7 10.1 %psum.14 = f32[136]{0:T(256)S(1)} all-reduce(f32[136]{0:T(256)S(1)} %get-tuple-element.688), channel_id=1, replica_groups=mesh['section'=2,'seq'=32,'tensor'=4] {'tensor'}, use_global_device_ids=true, to_apply=%region_2.2 | all-reduce | flops 136 | bytes 1088 | tf_op jit(solution)/shard_map/while/body/eval_jaxpr/psum | solution.py:46
  479.8 23.4 %all-gather.6.cloned.1.call-done = bf16[136,4096]{1,0:T(8,128)(2,1)} async-done(((bf16[136,1024]{1,0:T(8,128)(2,1)}), bf16[136,4096]{1,0:T(8,128)(2,1)}) %all-gather.6.cloned.1.call-update) | async-done | bytes 1114128 | tf_op jit(solution)/shard_map/while/body/eval_jaxpr/all_gather | solution.py:49
  503.2 12.1 %convolution_convert_fusion.5 = bf16[136,3072]{1,0:T(8,128)(2,1)S(1)} fusion(bf16[136,4096]{1,0:T(8,128)(2,1)} %all-gather.6.cloned.1.call-done, bf16[4096,3072]{1,0:T(8,128)(2,1)} %get-tuple-element.867), kind=kOutput, calls=%fused_computation.2.clone.1 | convolution fusion | flops 3422969856 | bytes 27115520 | tf_op jit(solution)/shard_map/while/body/eval_jaxpr/dot_general | solution.py:42
  515.4 1.9 collective-permute-start
  518.1 1.2 reshape.29
  519.3 3.7 collective-permute-done
  523.6 4.2 fusion.174
  530.0 1.9 collective-permute-start.1
  532.1 7.7 %collective-permute-done.1 = bf16[127,1024]{1,0:T(8,128)(2,1)S(1)} collective-permute-done((bf16[127,1024]{1,0:T(8,128)(2,1)S(1)}, bf16[127,1024]{1,0:T(8,128)(2,1)S(1)}, u32[]{:S(2)}, u32[]{:S(2)}) %collective-permute-start.1) | collective-permute-done | bytes 260128 | tf_op jit(solution)/shard_map/while/body/eval_jaxpr/ppermute | solution.py:12
  540.3 16.9 %convolution_convert_fusion.6 = bf16[136,4096]{1,0:T(8,128)(2,1)} fusion(bf16[1024,4096]{1,0:T(8,128)(2,1)} %get-tuple-element.869, f32[263,1024]{1,0:T(8,128)S(1)} %maximum_convert_fusion.5, f32[1024]{0:T(1024)S(1)} %bitcast.458, f32[1024]{0:T(1024)S(1)} %bitcast.459, f32[1024]{0:T(1024)S(1)} %bitcast.460, f32[1024]{0:T(1024)S(1)} %bitcast.461, ...), kind=kOutput, calls=%fused_computation.1.clone.1 | convolution fusion | flops 1177198592 | bytes 81887232 | tf_op jit(solution)/shard_map/while/body/eval_jaxpr/dot_general | solution.py:60
  557.3 24.3 %reduce-scatter.2.cloned.1.call-done = bf16[136,1024]{1,0:T(8,128)(2,1)} async-done(((bf16[136,4096]{1,0:T(8,128)(2,1)}), bf16[136,1024]{1,0:T(8,128)(2,1)}) %reduce-scatter.2.cloned.1.call-update) | async-done | bytes 278544 | tf_op jit(solution)/shard_map/while/body/eval_jaxpr/reduce_scatter | solution.py:61
  582.7 1.3 collective-permute-start.2
  584.0 9.4 %collective-permute-done.2 = bf16[136,1024]{1,0:T(8,128)(2,1)S(1)} collective-permute-done((bf16[136,1024]{1,0:T(8,128)(2,1)S(1)}, bf16[136,1024]{1,0:T(8,128)(2,1)S(1)}, u32[]{:S(2)}, u32[]{:S(2)}) %collective-permute-start.2) | collective-permute-done | bytes 278560 | tf_op jit(solution)/shard_map/while/body/eval_jaxpr/ppermute | solution.py:12
  (333 shorter events, 25.1 us)
Async XLA Ops:
  6.5 168.0 %all-gather.4.cloned.1.call-start = ((), (), s32[]{:S(2)}) async-start(), calls=%async_computation.1 | async-start | bytes 25952256 | tf_op jit(solution)/shard_map/all_gather | solution.py:39
  174.6 33.6 %copy-start.2 = (f32[1,128,1024]{2,1,0:T(8,128)S(1)}, f32[1,128,1024]{2,1,0:T(8,128)}, u32[]{:S(2)}) copy-start(f32[1,128,1024]{2,1,0:T(8,128)} %param.14) | copy-start | bytes 1572868
  208.2 36.5 %all-gather.6.cloned.1.call-start = ((), (), s32[]{:S(2)}) async-start(), calls=%async_computation.2 | async-start | bytes 1392640 | tf_op jit(solution)/shard_map/while/body/eval_jaxpr/all_gather | solution.py:49
  220.1 103.0 %reduce-scatter.2.cloned.1.call-start = ((), (), s32[]{:S(2)}) async-start(), calls=%async_computation.3 | async-start | bytes 1392640 | tf_op jit(solution)/shard_map/while/body/eval_jaxpr/reduce_scatter | solution.py:61
  256.9 7.5 %collective-permute-start = (bf16[6,3,1024]{2,1,0:T(4,128)(2,1)S(1)}, bf16[6,3,1024]{2,1,0:T(4,128)(2,1)S(1)}, u32[]{:S(2)}, u32[]{:S(2)}) collective-permute-start(bf16[6,3,1024]{2,1,0:T(4,128)(2,1)S(1)} %slice.4096), channel_id=1, source_target_pairs={{0,4},{4,8},{8,12},{12,16},{16,20},{20,24},{24,28},{28,32},{32,36}... | collective-permute-start | bytes 110600 | tf_op jit(solution)/shard_map/while/body/eval_jaxpr/ppermute | solution.py:12
  270.9 10.4 %copy-start.5 = (f32[1,1024]{1,0:T(1,128)S(1)}, f32[1,1024]{1,0:T(1,128)}, u32[]{:S(2)}) copy-start(f32[1,1024]{1,0:T(1,128)} %get-tuple-element.726) | copy-start | bytes 12292 | tf_op jit(solution)/shard_map/while
  271.0 10.4 %copy-start.6 = (f32[1,1024]{1,0:T(1,128)S(1)}, f32[1,1024]{1,0:T(1,128)}, u32[]{:S(2)}) copy-start(f32[1,1024]{1,0:T(1,128)} %get-tuple-element.727) | copy-start | bytes 12292 | tf_op jit(solution)/shard_map/while
  271.0 10.4 %copy-start.7 = (f32[1,1024]{1,0:T(1,128)S(1)}, f32[1,1024]{1,0:T(1,128)}, u32[]{:S(2)}) copy-start(f32[1,1024]{1,0:T(1,128)} %get-tuple-element.728) | copy-start | bytes 12292 | tf_op jit(solution)/shard_map/while
  271.0 10.4 %copy-start.8 = (f32[1,1024]{1,0:T(1,128)S(1)}, f32[1,1024]{1,0:T(1,128)}, u32[]{:S(2)}) copy-start(f32[1,1024]{1,0:T(1,128)} %get-tuple-element.729) | copy-start | bytes 12292 | tf_op jit(solution)/shard_map/while
  271.0 10.4 %copy-start.9 = (f32[1,1024]{1,0:T(1,128)S(1)}, f32[1,1024]{1,0:T(1,128)}, u32[]{:S(2)}) copy-start(f32[1,1024]{1,0:T(1,128)} %get-tuple-element.730) | copy-start | bytes 12292 | tf_op jit(solution)/shard_map/while
  271.0 10.4 %copy-start.10 = (f32[1,1024]{1,0:T(1,128)S(1)}, f32[1,1024]{1,0:T(1,128)}, u32[]{:S(2)}) copy-start(f32[1,1024]{1,0:T(1,128)} %get-tuple-element.731) | copy-start | bytes 12292 | tf_op jit(solution)/shard_map/while
  271.0 10.4 %copy-start.11 = (f32[1,1024]{1,0:T(1,128)S(1)}, f32[1,1024]{1,0:T(1,128)}, u32[]{:S(2)}) copy-start(f32[1,1024]{1,0:T(1,128)} %get-tuple-element.732) | copy-start | bytes 12292 | tf_op jit(solution)/shard_map/while
  271.0 10.4 %copy-start.12 = (f32[1,1024]{1,0:T(1,128)S(1)}, f32[1,1024]{1,0:T(1,128)}, u32[]{:S(2)}) copy-start(f32[1,1024]{1,0:T(1,128)} %get-tuple-element.822) | copy-start | bytes 12292 | tf_op jit(solution)/shard_map/while
  271.0 10.4 %copy-start.13 = (f32[1,1024]{1,0:T(1,128)S(1)}, f32[1,1024]{1,0:T(1,128)}, u32[]{:S(2)}) copy-start(f32[1,1024]{1,0:T(1,128)} %get-tuple-element.733) | copy-start | bytes 12292 | tf_op jit(solution)/shard_map/while
  271.0 10.4 %copy-start.14 = (f32[1,1024]{1,0:T(1,128)S(1)}, f32[1,1024]{1,0:T(1,128)}, u32[]{:S(2)}) copy-start(f32[1,1024]{1,0:T(1,128)} %get-tuple-element.734) | copy-start | bytes 12292 | tf_op jit(solution)/shard_map/while
  271.0 10.4 %copy-start.15 = (f32[1,1024]{1,0:T(1,128)S(1)}, f32[1,1024]{1,0:T(1,128)}, u32[]{:S(2)}) copy-start(f32[1,1024]{1,0:T(1,128)} %get-tuple-element.735) | copy-start | bytes 12292 | tf_op jit(solution)/shard_map/while
  271.1 10.4 %copy-start.16 = (f32[1,1024]{1,0:T(1,128)S(1)}, f32[1,1024]{1,0:T(1,128)}, u32[]{:S(2)}) copy-start(f32[1,1024]{1,0:T(1,128)} %get-tuple-element.736) | copy-start | bytes 12292 | tf_op jit(solution)/shard_map/while
  271.1 10.4 %copy-start.17 = (f32[1,1024]{1,0:T(1,128)S(1)}, f32[1,1024]{1,0:T(1,128)}, u32[]{:S(2)}) copy-start(f32[1,1024]{1,0:T(1,128)} %get-tuple-element.737) | copy-start | bytes 12292 | tf_op jit(solution)/shard_map/while
  271.1 10.4 %copy-start.18 = (f32[1,1024]{1,0:T(1,128)S(1)}, f32[1,1024]{1,0:T(1,128)}, u32[]{:S(2)}) copy-start(f32[1,1024]{1,0:T(1,128)} %get-tuple-element.738) | copy-start | bytes 12292 | tf_op jit(solution)/shard_map/while
  271.1 10.4 %copy-start.19 = (f32[1,1024]{1,0:T(1,128)S(1)}, f32[1,1024]{1,0:T(1,128)}, u32[]{:S(2)}) copy-start(f32[1,1024]{1,0:T(1,128)} %get-tuple-element.739) | copy-start | bytes 12292 | tf_op jit(solution)/shard_map/while
  271.1 10.4 %copy-start.20 = (f32[1,1024]{1,0:T(1,128)S(1)}, f32[1,1024]{1,0:T(1,128)}, u32[]{:S(2)}) copy-start(f32[1,1024]{1,0:T(1,128)} %get-tuple-element.740) | copy-start | bytes 12292 | tf_op jit(solution)/shard_map/while
  271.1 10.4 %copy-start.21 = (f32[1,1024]{1,0:T(1,128)S(1)}, f32[1,1024]{1,0:T(1,128)}, u32[]{:S(2)}) copy-start(f32[1,1024]{1,0:T(1,128)} %get-tuple-element.741) | copy-start | bytes 12292 | tf_op jit(solution)/shard_map/while
  271.1 10.4 %copy-start.22 = (f32[1,1024]{1,0:T(1,128)S(1)}, f32[1,1024]{1,0:T(1,128)}, u32[]{:S(2)}) copy-start(f32[1,1024]{1,0:T(1,128)} %get-tuple-element.742) | copy-start | bytes 12292 | tf_op jit(solution)/shard_map/while
  271.1 10.4 %copy-start.23 = (f32[1,1024]{1,0:T(1,128)S(1)}, f32[1,1024]{1,0:T(1,128)}, u32[]{:S(2)}) copy-start(f32[1,1024]{1,0:T(1,128)} %get-tuple-element.743) | copy-start | bytes 12292 | tf_op jit(solution)/shard_map/while
  271.1 10.4 %copy-start.24 = (f32[1,1024]{1,0:T(1,128)S(1)}, f32[1,1024]{1,0:T(1,128)}, u32[]{:S(2)}) copy-start(f32[1,1024]{1,0:T(1,128)} %get-tuple-element.744) | copy-start | bytes 12292 | tf_op jit(solution)/shard_map/while
  271.1 10.4 %copy-start.25 = (f32[1,1024]{1,0:T(1,128)S(1)}, f32[1,1024]{1,0:T(1,128)}, u32[]{:S(2)}) copy-start(f32[1,1024]{1,0:T(1,128)} %get-tuple-element.745) | copy-start | bytes 12292 | tf_op jit(solution)/shard_map/while
  271.2 10.4 %copy-start.26 = (f32[1,1024]{1,0:T(1,128)S(1)}, f32[1,1024]{1,0:T(1,128)}, u32[]{:S(2)}) copy-start(f32[1,1024]{1,0:T(1,128)} %get-tuple-element.746) | copy-start | bytes 12292 | tf_op jit(solution)/shard_map/while
  271.2 10.4 %copy-start.27 = (f32[1,1024]{1,0:T(1,128)S(1)}, f32[1,1024]{1,0:T(1,128)}, u32[]{:S(2)}) copy-start(f32[1,1024]{1,0:T(1,128)} %get-tuple-element.747) | copy-start | bytes 12292 | tf_op jit(solution)/shard_map/while
  271.2 10.4 %copy-start.28 = (f32[1,1024]{1,0:T(1,128)S(1)}, f32[1,1024]{1,0:T(1,128)}, u32[]{:S(2)}) copy-start(f32[1,1024]{1,0:T(1,128)} %get-tuple-element.748) | copy-start | bytes 12292 | tf_op jit(solution)/shard_map/while
  271.2 10.4 %copy-start.29 = (f32[1,1024]{1,0:T(1,128)S(1)}, f32[1,1024]{1,0:T(1,128)}, u32[]{:S(2)}) copy-start(f32[1,1024]{1,0:T(1,128)} %get-tuple-element.749) | copy-start | bytes 12292 | tf_op jit(solution)/shard_map/while
  271.4 9.8 %collective-permute-start.1 = (bf16[127,1024]{1,0:T(8,128)(2,1)S(1)}, bf16[127,1024]{1,0:T(8,128)(2,1)S(1)}, u32[]{:S(2)}, u32[]{:S(2)}) collective-permute-start(bf16[127,1024]{1,0:T(8,128)(2,1)S(1)} %bitcast.453), channel_id=1, source_target_pairs={{0,4},{4,8},{8,12},{12,16},{16,20},{20,24},{24,28},{28,32},{32,36}... | collective-permute-start | bytes 780296 | tf_op jit(solution)/shard_map/while/body/eval_jaxpr/ppermute | solution.py:12
  281.7 17.0 %copy-start.3 = (bf16[2,136,1024]{2,1,0:T(8,128)(2,1)S(1)}, bf16[2,136,1024]{2,1,0:T(8,128)(2,1)}, u32[]{:S(2)}) copy-start(bf16[2,136,1024]{2,1,0:T(8,128)(2,1)} %get-tuple-element.845) | copy-start | bytes 1671172 | tf_op jit(solution)/shard_map/while
  324.2 10.8 %copy-start.4 = (bf16[2,136,1024]{2,1,0:T(8,128)(2,1)}, bf16[2,136,1024]{2,1,0:T(8,128)(2,1)S(1)}, u32[]{:S(2)}) copy-start(bf16[2,136,1024]{2,1,0:T(8,128)(2,1)S(1)} %get-tuple-element.860) | copy-start | bytes 1671172 | tf_op jit(solution)/shard_map/while
  324.2 10.8 %collective-permute-start.2 = (bf16[136,1024]{1,0:T(8,128)(2,1)S(1)}, bf16[136,1024]{1,0:T(8,128)(2,1)S(1)}, u32[]{:S(2)}, u32[]{:S(2)}) collective-permute-start(bf16[136,1024]{1,0:T(8,128)(2,1)S(1)} %get-tuple-element.826), channel_id=1, source_target_pairs={{0,128},{1,129},{2,130},{3,131},{4,132},{5,133},{6,134},{7,135},{8... | collective-permute-start | bytes 835592 | tf_op jit(solution)/shard_map/while/body/eval_jaxpr/ppermute | solution.py:12
  335.0 38.9 %all-gather.6.cloned.1.call-start = ((), (), s32[]{:S(2)}) async-start(), calls=%async_computation.2 | async-start | bytes 1392640 | tf_op jit(solution)/shard_map/while/body/eval_jaxpr/all_gather | solution.py:49
  348.3 104.0 %reduce-scatter.2.cloned.1.call-start = ((), (), s32[]{:S(2)}) async-start(), calls=%async_computation.3 | async-start | bytes 1392640 | tf_op jit(solution)/shard_map/while/body/eval_jaxpr/reduce_scatter | solution.py:61
  386.2 7.5 %collective-permute-start = (bf16[6,3,1024]{2,1,0:T(4,128)(2,1)S(1)}, bf16[6,3,1024]{2,1,0:T(4,128)(2,1)S(1)}, u32[]{:S(2)}, u32[]{:S(2)}) collective-permute-start(bf16[6,3,1024]{2,1,0:T(4,128)(2,1)S(1)} %slice.4096), channel_id=1, source_target_pairs={{0,4},{4,8},{8,12},{12,16},{16,20},{20,24},{24,28},{28,32},{32,36}... | collective-permute-start | bytes 110600 | tf_op jit(solution)/shard_map/while/body/eval_jaxpr/ppermute | solution.py:12
  400.7 9.8 %collective-permute-start.1 = (bf16[127,1024]{1,0:T(8,128)(2,1)S(1)}, bf16[127,1024]{1,0:T(8,128)(2,1)S(1)}, u32[]{:S(2)}, u32[]{:S(2)}) collective-permute-start(bf16[127,1024]{1,0:T(8,128)(2,1)S(1)} %bitcast.453), channel_id=1, source_target_pairs={{0,4},{4,8},{8,12},{12,16},{16,20},{20,24},{24,28},{28,32},{32,36}... | collective-permute-start | bytes 780296 | tf_op jit(solution)/shard_map/while/body/eval_jaxpr/ppermute | solution.py:12
  411.0 17.0 %copy-start.3 = (bf16[2,136,1024]{2,1,0:T(8,128)(2,1)S(1)}, bf16[2,136,1024]{2,1,0:T(8,128)(2,1)}, u32[]{:S(2)}) copy-start(bf16[2,136,1024]{2,1,0:T(8,128)(2,1)} %get-tuple-element.845) | copy-start | bytes 1671172 | tf_op jit(solution)/shard_map/while
  453.4 10.9 %copy-start.4 = (bf16[2,136,1024]{2,1,0:T(8,128)(2,1)}, bf16[2,136,1024]{2,1,0:T(8,128)(2,1)S(1)}, u32[]{:S(2)}) copy-start(bf16[2,136,1024]{2,1,0:T(8,128)(2,1)S(1)} %get-tuple-element.860) | copy-start | bytes 1671172 | tf_op jit(solution)/shard_map/while
  453.4 10.9 %collective-permute-start.2 = (bf16[136,1024]{1,0:T(8,128)(2,1)S(1)}, bf16[136,1024]{1,0:T(8,128)(2,1)S(1)}, u32[]{:S(2)}, u32[]{:S(2)}) collective-permute-start(bf16[136,1024]{1,0:T(8,128)(2,1)S(1)} %get-tuple-element.826), channel_id=1, source_target_pairs={{0,128},{1,129},{2,130},{3,131},{4,132},{5,133},{6,134},{7,135},{8... | collective-permute-start | bytes 835592 | tf_op jit(solution)/shard_map/while/body/eval_jaxpr/ppermute | solution.py:12
  464.3 38.9 %all-gather.6.cloned.1.call-start = ((), (), s32[]{:S(2)}) async-start(), calls=%async_computation.2 | async-start | bytes 1392640 | tf_op jit(solution)/shard_map/while/body/eval_jaxpr/all_gather | solution.py:49
  477.6 104.0 %reduce-scatter.2.cloned.1.call-start = ((), (), s32[]{:S(2)}) async-start(), calls=%async_computation.3 | async-start | bytes 1392640 | tf_op jit(solution)/shard_map/while/body/eval_jaxpr/reduce_scatter | solution.py:61
  515.4 7.5 %collective-permute-start = (bf16[6,3,1024]{2,1,0:T(4,128)(2,1)S(1)}, bf16[6,3,1024]{2,1,0:T(4,128)(2,1)S(1)}, u32[]{:S(2)}, u32[]{:S(2)}) collective-permute-start(bf16[6,3,1024]{2,1,0:T(4,128)(2,1)S(1)} %slice.4096), channel_id=1, source_target_pairs={{0,4},{4,8},{8,12},{12,16},{16,20},{20,24},{24,28},{28,32},{32,36}... | collective-permute-start | bytes 110600 | tf_op jit(solution)/shard_map/while/body/eval_jaxpr/ppermute | solution.py:12
  530.0 9.8 %collective-permute-start.1 = (bf16[127,1024]{1,0:T(8,128)(2,1)S(1)}, bf16[127,1024]{1,0:T(8,128)(2,1)S(1)}, u32[]{:S(2)}, u32[]{:S(2)}) collective-permute-start(bf16[127,1024]{1,0:T(8,128)(2,1)S(1)} %bitcast.453), channel_id=1, source_target_pairs={{0,4},{4,8},{8,12},{12,16},{16,20},{20,24},{24,28},{28,32},{32,36}... | collective-permute-start | bytes 780296 | tf_op jit(solution)/shard_map/while/body/eval_jaxpr/ppermute | solution.py:12
  540.3 17.0 %copy-start.3 = (bf16[2,136,1024]{2,1,0:T(8,128)(2,1)S(1)}, bf16[2,136,1024]{2,1,0:T(8,128)(2,1)}, u32[]{:S(2)}) copy-start(bf16[2,136,1024]{2,1,0:T(8,128)(2,1)} %get-tuple-element.845) | copy-start | bytes 1671172 | tf_op jit(solution)/shard_map/while
  582.7 10.8 %copy-start.4 = (bf16[2,136,1024]{2,1,0:T(8,128)(2,1)}, bf16[2,136,1024]{2,1,0:T(8,128)(2,1)S(1)}, u32[]{:S(2)}) copy-start(bf16[2,136,1024]{2,1,0:T(8,128)(2,1)S(1)} %get-tuple-element.860) | copy-start | bytes 1671172 | tf_op jit(solution)/shard_map/while
  582.7 10.7 %collective-permute-start.2 = (bf16[136,1024]{1,0:T(8,128)(2,1)S(1)}, bf16[136,1024]{1,0:T(8,128)(2,1)S(1)}, u32[]{:S(2)}, u32[]{:S(2)}) collective-permute-start(bf16[136,1024]{1,0:T(8,128)(2,1)S(1)} %get-tuple-element.826), channel_id=1, source_target_pairs={{0,128},{1,129},{2,130},{3,131},{4,132},{5,133},{6,134},{7,135},{8... | collective-permute-start | bytes 835592 | tf_op jit(solution)/shard_map/while/body/eval_jaxpr/ppermute | solution.py:12
  (95 other events, 962.8 us)
Sparse Core Ops, SparseCore 0:
  9.1 165.3 all-gather.3
  220.2 24.4 all-gather.5
  298.8 24.2 reduce-scatter.1
  348.4 25.4 all-gather.5
  428.1 24.2 reduce-scatter.1
  477.7 25.4 all-gather.5
  557.4 24.2 reduce-scatter.1
where the time goes:
time: 605 us; the launch traced here: 601 us
  waiting for transfers between devices  370 us (61%)
  matrix products  92.2 us (15%)
  local copies, waits for them, and re-layouts  54 us (9%)
  blocking collectives  28.7 us (5%)
  other arithmetic  24.1 us (4%)
  starting transfers between devices  15.6 us (3%)
  between operations  13.4 us (2%)
    all_gather x1, waiting for transfers between devices, body(): lax.all_gather(in_weight[0], 'seq', axis=0, tiled=True)  166 us
    reduce_scatter x3, waiting for transfers between devices, section_layer(): lax.psum_scatter(partial_terms.astype(jnp.bfloat16), 'tensor', scatter_di...  72.9 us
    all_gather x3, waiting for transfers between devices, section_layer(): proj_sum = project_in(lax.all_gather(normed, 'tensor', axis=1, tiled=True))  69.3 us
    ppermute x9, waiting for transfers between devices, passed_along(): lax.ppermute(value, axis, [(source, source + steps) for source in range(i...  62.6 us
    dot_general x3, matrix products, section_layer(): partial_terms = jnp.dot(mixed, weight, preferred_element_type=jnp.float32)  50.7 us
    dot_general x3, matrix products, project_in(): return jnp.dot(piece, in_full, preferred_element_type=jnp.float32)  36.4 us
    unnamed x11, local copies, waits for them, and re-layouts  35.8 us
    psum x3, blocking collectives, section_layer(): squares = lax.psum(jnp.sum(values * values, axis=1), 'tensor')  28.7 us
  transfers between devices with their start and end apart: 16, of which 16 were waited for; matrix products, arithmetic and copies ran while one was open for 2% of the time, Pallas kernels for 0%

commit v1 on v0

v1 whole, which is shorter than its diff:
```python
import functools

import jax
import jax.numpy as jnp
from jax import lax
from jax.experimental import pallas as pl
from jax.experimental.pallas import tpu as pltpu
from jax.sharding import PartitionSpec as P

EPS = 1e-06
MESH = pl.DeviceIdType.MESH
RING = 8
VMEM = pl.BlockSpec(memory_space=pltpu.VMEM)
HBM = pl.BlockSpec(memory_space=pltpu.HBM)


def place():
    seq = lax.axis_index("seq")
    return seq // (2 * RING), (seq // 2) % RING, seq % 2


def seq_of(y, z, core):
    return (y * RING + z) * 2 + core


class Gather:
    MOVES = (
        ("a1", "up", True, 0, None),
        ("b1", "down", True, 0, None),
        ("c1", "y", True, 0, None),
        ("a2", "up", True, -1, None),
        ("b2", "down", True, 1, None),
        ("a3", "up", True, -2, None),
        ("b3", "down", True, 2, None),
        ("c2", "y", True, -2, 1),
        ("c3", "y", True, 2, 0),
        ("a4", "up", True, -3, 0),
        ("b4", "down", True, 3, 1),
        ("a5", "up", False, 0, None),
        ("b5", "down", False, 0, None),
        ("c4", "y", True, -3, None),
        ("c5", "y", True, 3, None),
        ("a6", "up", False, -1, 0),
        ("b6", "down", False, 1, 1),
        ("c6", "y", True, 4, 0),
        ("c7", "y", True, 4, 1),
    )
    COUNT = len(MOVES)

    def __init__(self, slot, own, send, recv, side_send, side_recv):
        self.y, self.z, self.core = place()
        self.slot, self.own = slot, own
        self.send, self.recv = send, recv
        self.side_send, self.side_recv = side_send, side_recv
        self.index = {move[0]: at for at, move in enumerate(self.MOVES)}
        self.pending = []

    def target(self, direction):
        if direction == "up":
            return seq_of(self.y, (self.z + 1) % RING, self.core)
        if direction == "down":
            return seq_of(self.y, (self.z + RING - 1) % RING, self.core)
        return seq_of(1 - self.y, self.z, self.core)

    def block(self, same, dz, core=None):
        y = self.y if same else 1 - self.y
        return seq_of(y, (self.z + dz + RING) % RING, self.core if core is None else core)

    def copy(self, name):
        at = self.index[name]
        _, direction, same, dz, half = self.MOVES[at]
        block = self.block(same, dz)
        dst = self.slot(block, half)
        src = self.own if same and dz == 0 else dst
        return pltpu.make_async_remote_copy(
            src_ref=src,
            dst_ref=dst,
            send_sem=self.send.at[at],
            recv_sem=self.recv.at[at],
            device_id={"seq": self.target(direction)},
            device_id_type=MESH,
        )

    def start(self, *names):
        for name in names:
            self.copy(name).start()

    def landed(self, name):
        at = self.index[name]
        _, direction, same, dz, half = self.MOVES[at]
        if direction == "y":
            block = self.block(not same, dz)
        else:
            block = self.block(same, dz + (-1 if direction == "up" else 1))
        got = self.slot(block, half)
        pltpu.make_async_copy(got, got, self.recv.at[at]).wait()
        side = pltpu.make_async_remote_copy(
            src_ref=got,
            dst_ref=got,
            send_sem=self.side_send.at[at],
            recv_sem=self.side_recv.at[at],
            device_id={"seq": seq_of(self.y, self.z, 1 - self.core)},
            device_id_type=MESH,
        )
        side.start()

    def side_own(self):
        return pltpu.make_async_remote_copy(
            src_ref=self.own,
            dst_ref=self.slot(self.block(True, 0), None),
            send_sem=self.side_send.at[self.COUNT],
            recv_sem=self.side_recv.at[self.COUNT],
            device_id={"seq": seq_of(self.y, self.z, 1 - self.core)},
            device_id_type=MESH,
        )

    def run(self, local_sem):
        keep = pltpu.make_async_copy(self.own, self.slot(self.block(True, 0), None), local_sem)
        self.start("a1", "b1", "c1")
        self.side_own().start()
        keep.start()
        self.landed("a1")
        self.start("a2")
        self.landed("b1")
        self.start("b2")
        self.landed("c1")
        self.landed("a2")
        self.start("a3", "c2")
        self.landed("b2")
        self.start("b3", "c3")
        self.start("a5", "b5")
        self.landed("a3")
        self.start("a4", "c4")
        self.landed("b3")
        self.start("b4", "c5")
        self.landed("a5")
        self.start("a6")
        self.landed("b5")
        self.start("b6")
        self.landed("a4")
        self.start("c6")
        self.landed("b4")
        self.start("c7")
        for name in ("c2", "c3", "a6", "b6", "c4", "c5", "c6", "c7"):
            self.landed(name)
        keep.wait()
        for at, (name, direction, same, dz, half) in enumerate(self.MOVES):
            self.copy(name).wait_send()
            if direction == "y":
                block = (not same, dz)
            else:
                block = (same, dz + (-1 if direction == "up" else 1))
            mine = self.slot(self.block(*block), half)
            pltpu.make_async_copy(mine, mine, self.side_send.at[at]).wait()
            other = self.slot(self.block(*block, 1 - self.core), half)
            pltpu.make_async_copy(other, other, self.side_recv.at[at]).wait()
        side = self.side_own()
        side.wait_send()
        other = self.slot(self.block(True, 0, 1 - self.core), None)
        pltpu.make_async_copy(other, other, self.side_recv.at[self.COUNT]).wait()


def first_kernel(
    tail, shard, table, gain, t_full, w_full, tail_all, part, tables,
    send, recv, side_send, side_recv, a2a_send, a2a_recv, x_send, x_recv, local,
):
    section = lax.axis_index("section")
    tensor = lax.axis_index("tensor")
    seq = lax.axis_index("seq")
    y, z, core = place()
    count = tail.shape[0]
    share, depth = tail.shape[1], tail.shape[2]
    vocab, width = table.shape
    half = vocab // 2
    ways = tables.shape[0]
    barrier = pltpu.get_barrier_semaphore()

    def greet(**axes):
        pl.semaphore_signal(barrier, inc=1, device_id=axes, device_id_type=MESH)

    @pl.when(section == 1)
    def _():
        greet(seq=seq_of(y, (z + 1) % RING, core))
        greet(seq=seq_of(y, (z + RING - 1) % RING, core))
        greet(seq=seq_of(1 - y, z, core))
        greet(seq=seq_of(y, z, 1 - core))
        pl.semaphore_wait(barrier, 4)

        def slot(block, part_of):
            if part_of is None:
                return w_full.at[pl.ds(pl.multiple_of(block * depth, depth), depth)]
            rows = depth // 2
            return w_full.at[pl.ds(pl.multiple_of(block * depth + part_of * rows, rows), rows)]

        Gather(slot, shard, send, recv, side_send, side_recv).run(local.at[0])

    @pl.when(section == 0)
    def _():
        right, left = (tensor + 1) % ways, (tensor + ways - 1) % ways
        greet(tensor=right)
        greet(tensor=left)

        def greet_seq(step, carry):
            greet(seq=(seq + step) % count)
            return carry

        lax.fori_loop(1, count, greet_seq, 0)
        pl.semaphore_wait(barrier, count + 1)

        rows = pl.ds(pl.multiple_of(core * half, half), half)

        def along(at, src, owner, to):
            return pltpu.make_async_remote_copy(
                src_ref=src,
                dst_ref=tables.at[owner, rows],
                send_sem=x_send.at[at],
                recv_sem=x_recv.at[at],
                device_id={"tensor": to},
                device_id_type=MESH,
            )

        def across(at, owner):
            return pltpu.make_async_remote_copy(
                src_ref=tables.at[owner, rows],
                dst_ref=tables.at[owner, rows],
                send_sem=x_send.at[at],
                recv_sem=x_recv.at[at],
                device_id={"seq": seq_of(y, z, 1 - core)},
                device_id_type=MESH,
            )

        mine = table.at[rows]
        along(0, mine, tensor, right).start()
        along(1, mine, tensor, left).start()
        keep = pltpu.make_async_copy(table, tables.at[tensor], local.at[0])
        keep.start()

        def spread(step):
            to = (seq + step) % count
            return pltpu.make_async_remote_copy(
                src_ref=tail.at[to],
                dst_ref=tail_all.at[:, pl.ds(pl.multiple_of(seq * depth, depth), depth)],
                send_sem=a2a_send.at[step],
                recv_sem=a2a_recv.at[step],
                device_id={"seq": to},
                device_id_type=MESH,
            )

        def spread_start(step, carry):
            spread(step).start()
            return carry

        lax.fori_loop(1, count, spread_start, 0)
        keep_tail = pltpu.make_async_copy(
            tail.at[seq],
            tail_all.at[:, pl.ds(pl.multiple_of(seq * depth, depth), depth)],
            local.at[1],
        )
        keep_tail.start()

        far = (tensor + 2) % ways
        along(0, mine, tensor, right).wait_recv()
        across(3, left).start()
        along(1, mine, tensor, left).wait_recv()
        across(4, right).start()

        @pl.when(core == 0)
        def _():
            along(2, tables.at[left, rows], left, right).start()

        @pl.when(core == 1)
        def _():
            along(2, tables.at[right, rows], right, left).start()

        got = tables.at[far, rows]
        pltpu.make_async_copy(got, got, x_recv.at[2]).wait()
        across(5, far).start()
        keep.wait()
        for at, owner in ((3, left), (4, right), (5, far)):
            across(at, owner).wait_recv()
        along(0, mine, tensor, right).wait_send()
        along(1, mine, tensor, left).wait_send()
        pltpu.make_async_copy(got, got, x_send.at[2]).wait()
        for at, owner in ((3, left), (4, right), (5, far)):
            across(at, owner).wait_send()

        lines = 32

        def normalise(at, carry):
            window = pl.ds(pl.multiple_of(at * lines, lines), lines)
            total = jnp.zeros((lines, 1), jnp.float32)
            for way in range(ways):
                values = tables[way, window, :].astype(jnp.float32)
                total += jnp.sum(values * values, axis=1, keepdims=True)
            scale = lax.rsqrt(total / (ways * width) + EPS)
            for way in range(ways):
                values = tables[way, window, :].astype(jnp.float32)
                values = values * scale * gain[:, way * width : (way + 1) * width]
                tables[way, window, :] = values.astype(jnp.bfloat16)
            return carry

        lax.fori_loop(0, vocab // lines, normalise, 0)

        def spread_wait(step, carry):
            spread(step).wait_send()
            piece = tail_all.at[:, pl.ds(0, depth)]
            pltpu.make_async_copy(piece, piece, a2a_recv.at[step]).wait()
            return carry

        lax.fori_loop(1, count, spread_wait, 0)
        keep_tail.wait()
        total = jnp.zeros((share, vocab), jnp.float32)
        for way in range(ways):
            total += lax.dot_general(
                tail_all[:, way * width : (way + 1) * width],
                tables[way],
                (((1,), (1,)), ((), ())),
                preferred_element_type=jnp.float32,
            )
        wide = part.shape[1]
        for stream in range(3):
            part[stream] = total[stream * wide : (stream + 1) * wide].astype(jnp.bfloat16)

        def slot(block, part_of):
            if part_of is None:
                return t_full.at[:, pl.ds(pl.multiple_of(block * wide, wide), wide)]
            rows_of = wide // 2
            at = pl.multiple_of(block * wide + part_of * rows_of, rows_of)
            return t_full.at[:, pl.ds(at, rows_of)]

        Gather(slot, part, send, recv, side_send, side_recv).run(local.at[0])


def prepare(tail, shard, table, gain):
    count, share, depth = tail.shape
    vocab, width = table.shape
    full = gain.shape[1]
    moves = Gather.COUNT
    dma = pltpu.SemaphoreType.DMA
    return pl.pallas_call(
        first_kernel,
        out_shape=(
            jax.ShapeDtypeStruct((3, width, vocab), jnp.bfloat16),
            jax.ShapeDtypeStruct((full, 3 * width), jnp.bfloat16),
        ),
        in_specs=[VMEM, HBM, VMEM, VMEM],
        out_specs=(HBM, HBM),
        scratch_shapes=[
            pltpu.VMEM((share, full), jnp.bfloat16),
            pltpu.VMEM((3, share // 3, vocab), jnp.bfloat16),
            pltpu.VMEM((full // width, vocab, width), jnp.bfloat16),
            dma((moves,)),
            dma((moves,)),
            dma((moves + 1,)),
            dma((moves + 1,)),
            dma((count,)),
            dma((count,)),
            dma((6,)),
            dma((6,)),
            dma((2,)),
        ],
        compiler_params=pltpu.CompilerParams(
            collective_id=0, has_side_effects=True, vmem_limit_bytes=24 << 20
        ),
        name="prepare",
    )(tail, shard, table, gain)


def passed_along(value, axis, steps):
    count = lax.axis_size(axis)
    initial, last = (max(0, -steps), min(count, count - steps))
    return lax.ppermute(value, axis, [(source, source + steps) for source in range(initial, last)])


def causal_sum(extended, coeffs, length):
    taps = coeffs.shape[0]
    total = jnp.zeros((extended.shape[0], length) + extended.shape[2:], jnp.float32)
    for tap in range(taps):
        begin = taps - 1 - tap
        total = total + coeffs[tap][None, None] * extended[:, begin : begin + length]
    return total


def body(token_ids, embed_table, norm_gain, in_weight, se_filter, mr_filter, out_weight):
    micro, length = token_ids.shape
    vocab, width = embed_table.shape
    full = norm_gain.shape[1]
    section = lax.axis_index("section")
    seq = lax.axis_index("seq")
    gain = norm_gain[0]
    short_coeffs = jnp.transpose(se_filter[0], (1, 0, 2))
    medium_taps = mr_filter[0]
    weight = out_weight[0]
    se = short_coeffs.shape[0] - 1
    mr = medium_taps.shape[0] - 1
    count = lax.axis_size("seq")
    shard = in_weight[0].reshape(-1, 3 * width)
    tail = in_weight[0].reshape(-1, 3, count, width // count).transpose(2, 1, 3, 0)
    tail = tail.reshape(count, 3 * width // count, -1)
    projected_table, in_full = prepare(tail, shard, embed_table, norm_gain)
    projected_table = projected_table.reshape(3 * width, vocab)

    def normalised(rows):
        values = rows.astype(jnp.float32)
        scale = lax.rsqrt(jnp.mean(values * values, axis=1) + EPS)
        return (values * scale[:, None] * gain[None, :]).astype(jnp.bfloat16)

    def finish(values, query, gated_ext):
        medium = causal_sum(gated_ext.astype(jnp.float32), medium_taps, length)
        mixed = (query * medium).astype(jnp.bfloat16).reshape(micro * length, width)
        terms = jnp.dot(mixed, weight, preferred_element_type=jnp.float32)
        projected = lax.psum_scatter(
            terms.astype(jnp.bfloat16), "tensor", scatter_dimension=1, tiled=True
        ).astype(jnp.float32)
        return (values.astype(jnp.float32) + projected).astype(jnp.bfloat16)

    before = passed_along(token_ids + 1, "seq", 1) - 1
    ids = jnp.concatenate([before, token_ids], axis=1).reshape(-1)
    onehot = (ids[:, None] == jnp.arange(vocab, dtype=jnp.int32)[None, :]).astype(jnp.bfloat16)
    streams = (
        lax.dot_general(
            onehot, projected_table, (((1,), (1,)), ((), ())), preferred_element_type=jnp.float32
        )
        .astype(jnp.bfloat16)
        .reshape(micro, 2 * length, 3, width)
    )
    own = onehot.reshape(micro, 2 * length, vocab)[:, length:].reshape(-1, vocab)
    stream_0 = jnp.dot(own, embed_table, preferred_element_type=jnp.float32).astype(jnp.bfloat16)
    wide = streams[:, length - mr - se :].astype(jnp.float32)
    reach = length + mr
    gated_ext = (
        causal_sum(wide[:, :, 1], short_coeffs[:, 1], reach)
        * causal_sum(wide[:, :, 2], short_coeffs[:, 2], reach)
    ).astype(jnp.bfloat16)
    query = causal_sum(wide[:, mr:, 0], short_coeffs[:, 0], length)
    stream_1 = finish(stream_0, query, gated_ext)
    arrived = passed_along(stream_1, "section", 1)

    normed = normalised(lax.all_gather(arrived, "tensor", axis=1, tiled=True))
    streams = (
        jnp.dot(normed, in_full, preferred_element_type=jnp.float32)
        .astype(jnp.bfloat16)
        .reshape(micro, length, 3 * width)
    )
    rim = passed_along(streams[:, length - se :], "seq", 1)
    reach = jnp.concatenate([rim, streams], axis=1).astype(jnp.float32)
    reach = reach.reshape(micro, length + se, 3, width)
    short = causal_sum(reach, short_coeffs, length)
    gated = (short[:, :, 1] * short[:, :, 2]).astype(jnp.bfloat16)
    second_rim = passed_along(gated[:, length - mr :], "seq", 1)
    stream_2 = finish(arrived, short[:, :, 0], jnp.concatenate([second_rim, gated], axis=1))
    result = jnp.where(section == 0, stream_1, stream_2)
    return result.reshape(1, micro, length, width)


def solution(mesh):
    in_specs = (
        P(None, "seq"),
        P(None, "tensor"),
        P("section", None),
        P("section", "seq", None, "tensor"),
        P("section", None, None, "tensor"),
        P("section", None, "tensor"),
        P("section", "tensor", None),
    )
    out_specs = P("section", None, "seq", "tensor")
    return jax.shard_map(body, mesh=mesh, in_specs=in_specs, out_specs=out_specs, check_vma=False)
```

time: 605 us -> 459 us (0.76)
  waiting for transfers between devices: 370 us -> 123 us
  Pallas kernels: 0 us -> 117 us
  other arithmetic: 24.1 us -> 85 us
  matrix products: 92.2 us -> 34.1 us
  blocking collectives: 28.7 us -> 0 us
  local copies, waits for them, and re-layouts: 54 us -> 67.1 us
  starting transfers between devices: 15.6 us -> 8.76 us
    all_gather x4 -> x1, waiting for transfers between devices: 235 us -> 34.5 us  [body(): normed = normalised(lax.all_gather(arrived, 'tensor', axis=1, tiled=True))]
    pallas_call x0 -> x1, Pallas kernels: none -> 117 us  [prepare(): pl.pallas_call(first_kernel, out_shape=(jax.ShapeDtypeStruct((3, width, v...]
    convert_element_type x9 -> x7, other arithmetic: 4.96 us -> 75.6 us  [the longest x2 60 us: finish(): mixed = (query * medium).astype(jnp.bfloat16).reshape(micro * length, width)]
    dot_general x9 -> x5, matrix products: 92.2 us -> 34.1 us  [the longest x2 14.4 us: finish(): terms = jnp.dot(mixed, weight, preferred_element_type=jnp.float32)]
    ppermute x9 -> x4, waiting for transfers between devices: 62.6 us -> 25.6 us  [passed_along(): lax.ppermute(value, axis, [(source, source + steps) for source in range(i...]
    psum x3 -> x0, blocking collectives: 28.7 us -> none  [section_layer(): squares = lax.psum(jnp.sum(values * values, axis=1), 'tensor')]
    slice x30 -> x15, local copies, waits for them, and re-layouts: 10.5 us -> 31.9 us  [the longest x10 15.1 us: causal_sum(): total = total + coeffs[tap][None, None] * extended[:, begin:begin + length]]
    unnamed x11 -> x195, local copies, waits for them, and re-layouts: 35.8 us -> 17.3 us
  transfers between devices with their start and end apart: 16 -> 7, of which waited for: 16 -> 5; matrix products, arithmetic and copies ran while one was open for 2% -> 5% of each run, Pallas kernels for 0% -> 26%
where the time goes in v1:
time: 459 us; the launch traced here: 450 us
  waiting for transfers between devices  123 us (27%)
  Pallas kernels  117 us (25%)
  other arithmetic  85 us (19%)
  local copies, waits for them, and re-layouts  67.1 us (15%)
  matrix products  34.1 us (7%)
  between operations  14.9 us (3%)
  starting transfers between devices  8.76 us (2%)
    pallas_call x1, Pallas kernels, prepare(): pl.pallas_call(first_kernel, out_shape=(jax.ShapeDtypeStruct((3, width, v...  117 us
    reduce_scatter x2, waiting for transfers between devices, finish(): lax.psum_scatter(terms.astype(jnp.bfloat16), 'tensor', scatter_dimension=...  63 us
    convert_element_type x2, other arithmetic, finish(): mixed = (query * medium).astype(jnp.bfloat16).reshape(micro * length, width)  60 us
    all_gather x1, waiting for transfers between devices, body(): normed = normalised(lax.all_gather(arrived, 'tensor', axis=1, tiled=True))  34.5 us
    ppermute x4, waiting for transfers between devices, passed_along(): lax.ppermute(value, axis, [(source, source + steps) for source in range(i...  25.6 us
    unnamed x195, local copies, waits for them, and re-layouts  17.3 us
    slice x10, local copies, waits for them, and re-layouts, causal_sum(): total = total + coeffs[tap][None, None] * extended[:, begin:begin + length]  15.1 us
    dot_general x2, matrix products, finish(): terms = jnp.dot(mixed, weight, preferred_element_type=jnp.float32)  14.4 us
  transfers between devices with their start and end apart: 7, of which 5 were waited for; matrix products, arithmetic and copies ran while one was open for 5% of the time, Pallas kernels for 26%

profile of v1, /device:TPU:26, one launch (start us, length us, event | category | flops | bytes accessed | tf_op | source)
XLA Modules:
  0.0 449.9 jit_solution(16833947116512603072)
XLA Ops:
  6.5 1.3 broadcast_add_fusion.1
  7.8 1.9 collective-permute-start
  9.7 1.8 fusion.315
  11.5 2.2 fusion.313
  13.7 2.0 fusion.312
  15.7 1.9 fusion.311
  17.6 2.0 fusion.310
  19.6 2.0 fusion.309
  21.6 2.0 fusion.314
  23.5 0.9 copy.59
  24.5 0.7 fusion.317
  25.1 0.6 fusion.318
  25.7 0.4 copy.28
  26.5 0.9 copy-done
  27.4 117.0 %prepare.1 = (bf16[3,1024,512]{2,1,0:T(8,128)(2,1)S(1)}, bf16[4096,3072]{1,0:T(8,128)(2,1)S(1)}) custom-call(bf16[32,96,128]{2,1,0:T(8,128)(2,1)S(1)} %bitcast.211, bf16[128,3072]{1,0:T(8,128)(2,1)S(1)} %copy.31.shard, bf16[512,1024]{1,0:T(8,128)(2,1)S(1)} %copy-done, f32[1,4096]{1,0:T(1,128)S(1)} %copy-done.1), custom_call_target="tpu_custom_call" | custom-call | tf_op jit(solution)/shard_map/prepare/pallas_call | solution.py:340
  144.4 8.3 %copy-done.2 = bf16[4096,3072]{1,0:T(8,128)(2,1)} copy-done((bf16[4096,3072]{1,0:T(8,128)(2,1)}, bf16[4096,3072]{1,0:T(8,128)(2,1)S(1)}, u32[]{:S(2)}) %copy-start.2) | copy-done | bytes 25165848
  152.7 1.6 copy-done.3
  154.4 0.7 broadcast_add_fusion
  155.2 5.6 %convolution_convert_fusion = bf16[544,3072]{1,0:T(8,128)(2,1)} fusion(bf16[3072,512]{1,0:T(8,128)(2,1)} %bitcast.213, s32[544]{0:T(1024)S(1)} %eq.29), kind=kOutput, calls=%fused_computation.8 | convolution fusion | flops 1713225728 | bytes 6490240 | tf_op jit(solution)/shard_map/dot_general | solution.py:421
  160.8 10.8 %reshape.353 = bf16[2,272,3,1024]{3,2,1,0:T(4,128)(2,1)} reshape(bf16[544,3072]{1,0:T(8,128)(2,1)} %convolution_convert_fusion) | data formatting | bytes 6684672 | tf_op jit(solution)/shard_map/reshape | solution.py:425
  171.6 8.2 %slice_convert_fusion = f32[2,269,3,1024]{3,2,1,0:T(4,128)} fusion(bf16[2,272,3,1024]{3,2,1,0:T(4,128)(2,1)} %reshape.353), kind=kLoop, calls=%fused_computation.12 | loop fusion | flops 1652736 | bytes 9916416 | tf_op jit(solution)/shard_map/convert_element_type | solution.py:429
  179.9 4.4 slice.2104
  184.3 12.1 %fusion.308 = (f32[2,269,1,1024]{3,2,1,0:T(1,128)S(1)}, f32[2,269,1,1024]{3,2,1,0:T(1,128)}) fusion(f32[2,269,3,1024]{3,2,1,0:T(4,128)} %slice_convert_fusion), kind=kLoop, calls=%fused_computation.615 | loop fusion | bytes 8814592 | tf_op jit(solution)/shard_map/slice | solution.py:432
  196.4 1.6 copy.58
  198.3 1.1 copy_bitcast_fusion
  199.8 5.0 %fusion.304 = f32[2,263,1024]{2,1,0:T(8,128)S(1)} fusion(f32[2,269,1024]{2,1,0:T(8,128)S(1)} %get-tuple-element.167, f32[1024]{0:T(1024)} %bitcast.486, f32[1024]{0:T(1024)} %bitcast.487, f32[1024]{0:T(1024)} %bitcast.488, f32[1024]{0:T(1024)} %bitcast.489, f32[1024]{0:T(1024)} %bitcast.490, f32[1024]{0:T(1024)} %bitcast.491, f32[1024]{0:T(1024)} %bitcast.492, ...), kind=kLoop, calls=%fused_computation.598 | loop fusion | flops 15620096 | bytes 32374784 | tf_op jit(solution)/shard_map/convert_element_type | solution.py:409
  205.2 31.7 %fusion.171 = bf16[2,136,1024]{2,1,0:T(8,128)(2,1)S(1)} fusion(f32[2,263,1024]{2,1,0:T(8,128)S(1)} %fusion.304, f32[1024]{0:T(1024)S(1)} %bitcast.249, f32[1024]{0:T(1024)S(1)} %bitcast.251, f32[1024]{0:T(1024)} %bitcast.407, f32[1024]{0:T(1024)} %bitcast.409, f32[1024]{0:T(1024)} %bitcast.411, f32[1024]{0:T(1024)} %bitcast.413, f32[1024]{0:T(1024)} %bitcast.415, ...), kind=kLoop, calls=%fused_computation.328 | loop fusion | flops 75202560 | bytes 151515136 | tf_op jit(solution)/shard_map/convert_element_type | solution.py:410
  236.9 7.2 %fusion.4 = bf16[272,4096]{1,0:T(8,128)(2,1)} fusion(bf16[272,1024]{1,0:T(8,128)(2,1)S(1)} %bitcast.222, bf16[1,1024,4096]{2,1,0:T(8,128)(2,1)} %param.13), kind=kOutput, calls=%fused_computation.6 | convolution fusion | flops 2282815488 | bytes 11173888 | tf_op jit(solution)/shard_map/dot_general | solution.py:411
  244.4 30.7 %reduce-scatter.3.cloned.1.call-done = bf16[272,1024]{1,0:T(8,128)(2,1)} async-done(((bf16[272,4096]{1,0:T(8,128)(2,1)}), bf16[272,1024]{1,0:T(8,128)(2,1)}) %reduce-scatter.3.cloned.1.call-update) | async-done | bytes 557072 | tf_op jit(solution)/shard_map/reduce_scatter | solution.py:412
  275.1 1.5 fusion.38
  276.6 0.8 copy-done.10
  277.4 1.3 collective-permute-start.1
  278.7 16.5 %collective-permute-done.1 = bf16[272,1024]{1,0:T(8,128)(2,1)S(1)} collective-permute-done((bf16[272,1024]{1,0:T(8,128)(2,1)S(1)}, bf16[272,1024]{1,0:T(8,128)(2,1)S(1)}, u32[]{:S(2)}, u32[]{:S(2)}) %collective-permute-start.1) | collective-permute-done | bytes 557088 | tf_op jit(solution)/shard_map/ppermute | solution.py:372
  295.2 0.8 copy-done.6
  296.2 34.5 %all-gather.2.cloned.1.call-done = bf16[272,4096]{1,0:T(8,128)(2,1)} async-done(((bf16[272,1024]{1,0:T(8,128)(2,1)}), bf16[272,4096]{1,0:T(8,128)(2,1)}) %all-gather.2.cloned.1.call-update) | async-done | bytes 2228240 | tf_op jit(solution)/shard_map/all_gather | solution.py:439
  330.7 2.3 fusion.10
  333.1 12.6 %convolution_convert_fusion.1 = bf16[272,3072]{1,0:T(8,128)(2,1)S(1)} fusion(bf16[4096,3072]{1,0:T(8,128)(2,1)} %copy-done.2, bf16[272,4096]{1,0:T(8,128)(2,1)S(1)} %copy-done.5, f32[4096]{0:T(1024)S(1)} %bitcast.212, f32[272]{0:T(512)S(1)} %add_rsqrt_fusion), kind=kOutput, calls=%fused_computation.13 | convolution fusion | flops 6850396160 | bytes 29082688 | tf_op jit(solution)/shard_map/dot_general | solution.py:441
  345.8 1.9 collective-permute-start.2
  347.7 4.8 %concatenate.16 = bf16[2,136,3,1024]{3,2,1,0:T(4,128)(2,1)S(1)} reshape(bf16[272,3072]{1,0:T(8,128)(2,1)} %copy-done.8) | data formatting | bytes 3342336 | tf_op jit(solution)/shard_map/concatenate | solution.py:446
  352.5 1.8 copy.34
  354.4 2.0 maximum_convert_fusion
  356.4 2.8 fusion.13
  359.8 3.6 collective-permute-start.3
  363.4 9.0 %collective-permute-done.3 = bf16[2,127,1024]{2,1,0:T(8,128)(2,1)S(1)} collective-permute-done((bf16[2,127,1024]{2,1,0:T(8,128)(2,1)S(1)}, bf16[2,127,1024]{2,1,0:T(8,128)(2,1)S(1)}, u32[]{:S(2)}, u32[]{:S(2)}) %collective-permute-start.3) | collective-permute-done | bytes 520224 | tf_op jit(solution)/shard_map/ppermute | solution.py:372
  373.1 28.4 %fusion.41 = bf16[2,136,1024]{2,1,0:T(8,128)(2,1)S(1)} fusion(f32[2,263,1024]{2,1,0:T(8,128)S(1)} %maximum_convert_fusion.1, f32[2,136,3,1024]{3,1,0,2:T(8,128)S(1)} %fusion.13, f32[1024]{0:T(1024)S(1)} %bitcast.250, f32[1024]{0:T(1024)S(1)} %bitcast.252, f32[1024]{0:T(1024)} %bitcast.408, f32[1024]{0:T(1024)} %bitcast.410, f32[1024]{0:T(1024)} %bitcast.412, ...), kind=kLoop, calls=%fused_computation.68 | loop fusion | flops 71581696 | bytes 144801792 | tf_op jit(solution)/shard_map/convert_element_type | solution.py:410
  401.5 7.2 %fusion.7 = bf16[272,4096]{1,0:T(8,128)(2,1)} fusion(bf16[272,1024]{1,0:T(8,128)(2,1)S(1)} %bitcast.221, bf16[1,1024,4096]{2,1,0:T(8,128)(2,1)} %param.13), kind=kOutput, calls=%fused_computation.7 | convolution fusion | flops 2282815488 | bytes 11173888 | tf_op jit(solution)/shard_map/dot_general | solution.py:411
  408.7 32.3 %reduce-scatter.5.cloned.1.call-done = bf16[272,1024]{1,0:T(8,128)(2,1)} async-done(((bf16[272,4096]{1,0:T(8,128)(2,1)}), bf16[272,1024]{1,0:T(8,128)(2,1)}) %reduce-scatter.5.cloned.1.call-update) | async-done | bytes 557072 | tf_op jit(solution)/shard_map/reduce_scatter | solution.py:412
  441.0 2.1 fusion.305
  (208 shorter events, 2.4 us)
Async XLA Ops:
  6.5 19.2 %copy-start.9 = (bf16[1,128,3,1024]{3,1,2,0:T(8,128)(2,1)S(1)}, bf16[1,128,3,1024]{3,1,2,0:T(8,128)(2,1)}, u32[]{:S(2)}) copy-start(bf16[1,128,3,1024]{3,1,2,0:T(8,128)(2,1)} %param.10) | copy-start | bytes 2359300
  6.5 268.5 %reduce-scatter.3.cloned.1.call-start = ((), (), s32[]{:S(2)}) async-start(), calls=%async_computation.2 | async-start | bytes 2785280 | tf_op jit(solution)/shard_map/reduce_scatter | solution.py:412
  7.8 146.5 %collective-permute-start = (s32[2,136]{1,0:T(2,128)}, s32[2,136]{1,0:T(2,128)}, u32[]{:S(2)}, u32[]{:S(2)}) collective-permute-start(s32[2,136]{1,0:T(2,128)} %broadcast_add_fusion.1), channel_id=1, source_target_pairs={{0,4},{4,8},{8,12},{12,16},{16,20},{20,24},{24,28},{28,32},{32,36}... | collective-permute-start | bytes 3272 | tf_op jit(solution)/shard_map/ppermute | solution.py:372
  27.4 127.6 %copy-start.92 = (s32[2,136]{1,0:T(2,128)S(1)}, s32[2,136]{1,0:T(2,128)}, u32[]{:S(2)}) copy-start(s32[2,136]{1,0:T(2,128)} %param.7) | copy-start | bytes 3268
  244.1 86.7 %all-gather.2.cloned.1.call-start = ((), (), s32[]{:S(2)}) async-start(), calls=%async_computation.3 | async-start | bytes 2785280 | tf_op jit(solution)/shard_map/all_gather | solution.py:439
  277.4 17.8 %collective-permute-start.1 = (bf16[272,1024]{1,0:T(8,128)(2,1)S(1)}, bf16[272,1024]{1,0:T(8,128)(2,1)S(1)}, u32[]{:S(2)}, u32[]{:S(2)}) collective-permute-start(bf16[272,1024]{1,0:T(8,128)(2,1)S(1)} %fusion.38), channel_id=1, source_target_pairs={{0,128},{1,129},{2,130},{3,131},{4,132},{5,133},{6,134},{7,135},{8... | collective-permute-start | bytes 1671176 | tf_op jit(solution)/shard_map/ppermute | solution.py:372
  296.1 144.9 %reduce-scatter.5.cloned.1.call-start = ((), (), s32[]{:S(2)}) async-start(), calls=%async_computation.4 | async-start | bytes 2785280 | tf_op jit(solution)/shard_map/reduce_scatter | solution.py:412
  345.8 8.5 %collective-permute-start.2 = (bf16[2,6,3072]{2,0,1:T(2,128)(2,1)S(1)}, bf16[2,6,3072]{2,0,1:T(2,128)(2,1)S(1)}, u32[]{:S(2)}, u32[]{:S(2)}) collective-permute-start(bf16[2,6,3072]{2,0,1:T(2,128)(2,1)S(1)} %copy.46), channel_id=1, source_target_pairs={{0,4},{4,8},{8,12},{12,16},{16,20},{20,24},{24,28},{28,32},{32,36}... | collective-permute-start | bytes 221192 | tf_op jit(solution)/shard_map/ppermute | solution.py:372
  359.4 13.2 %copy-start.45 = (f32[1,1,1024]{2,1,0:T(1,128)S(1)}, f32[1,1,1024]{2,1,0:T(1,128)}, u32[]{:S(2)}) copy-start(f32[1,1,1024]{2,1,0:T(1,128)} %get-tuple-element.75) | copy-start | bytes 12292
  359.5 13.2 %copy-start.47 = (f32[1,1,1024]{2,1,0:T(1,128)S(1)}, f32[1,1,1024]{2,1,0:T(1,128)}, u32[]{:S(2)}) copy-start(f32[1,1,1024]{2,1,0:T(1,128)} %get-tuple-element.76) | copy-start | bytes 12292
  359.5 13.2 %copy-start.49 = (f32[1,1,1024]{2,1,0:T(1,128)S(1)}, f32[1,1,1024]{2,1,0:T(1,128)}, u32[]{:S(2)}) copy-start(f32[1,1,1024]{2,1,0:T(1,128)} %get-tuple-element.77) | copy-start | bytes 12292
  359.5 13.2 %copy-start.51 = (f32[1,1,1024]{2,1,0:T(1,128)S(1)}, f32[1,1,1024]{2,1,0:T(1,128)}, u32[]{:S(2)}) copy-start(f32[1,1,1024]{2,1,0:T(1,128)} %get-tuple-element.78) | copy-start | bytes 12292
  359.5 13.2 %copy-start.53 = (f32[1,1,1024]{2,1,0:T(1,128)S(1)}, f32[1,1,1024]{2,1,0:T(1,128)}, u32[]{:S(2)}) copy-start(f32[1,1,1024]{2,1,0:T(1,128)} %get-tuple-element.79) | copy-start | bytes 12292
  359.5 13.2 %copy-start.55 = (f32[1,1,1024]{2,1,0:T(1,128)S(1)}, f32[1,1,1024]{2,1,0:T(1,128)}, u32[]{:S(2)}) copy-start(f32[1,1,1024]{2,1,0:T(1,128)} %get-tuple-element.80) | copy-start | bytes 12292
  359.5 13.2 %copy-start.57 = (f32[1,1,1024]{2,1,0:T(1,128)S(1)}, f32[1,1,1024]{2,1,0:T(1,128)}, u32[]{:S(2)}) copy-start(f32[1,1,1024]{2,1,0:T(1,128)} %get-tuple-element.81) | copy-start | bytes 12292
  359.5 13.2 %copy-start.59 = (f32[1,1,1024]{2,1,0:T(1,128)S(1)}, f32[1,1,1024]{2,1,0:T(1,128)}, u32[]{:S(2)}) copy-start(f32[1,1,1024]{2,1,0:T(1,128)} %get-tuple-element.82) | copy-start | bytes 12292
  359.5 13.2 %copy-start.60 = (f32[1,1,1024]{2,1,0:T(1,128)S(1)}, f32[1,1,1024]{2,1,0:T(1,128)}, u32[]{:S(2)}) copy-start(f32[1,1,1024]{2,1,0:T(1,128)} %get-tuple-element.83) | copy-start | bytes 12292
  359.5 13.2 %copy-start.61 = (f32[1,1,1024]{2,1,0:T(1,128)S(1)}, f32[1,1,1024]{2,1,0:T(1,128)}, u32[]{:S(2)}) copy-start(f32[1,1,1024]{2,1,0:T(1,128)} %get-tuple-element.84) | copy-start | bytes 12292
  359.5 13.2 %copy-start.62 = (f32[1,1,1024]{2,1,0:T(1,128)S(1)}, f32[1,1,1024]{2,1,0:T(1,128)}, u32[]{:S(2)}) copy-start(f32[1,1,1024]{2,1,0:T(1,128)} %get-tuple-element.85) | copy-start | bytes 12292
  359.6 13.2 %copy-start.63 = (f32[1,1,1024]{2,1,0:T(1,128)S(1)}, f32[1,1,1024]{2,1,0:T(1,128)}, u32[]{:S(2)}) copy-start(f32[1,1,1024]{2,1,0:T(1,128)} %get-tuple-element.86) | copy-start | bytes 12292
  359.6 13.2 %copy-start.64 = (f32[1,1,1024]{2,1,0:T(1,128)S(1)}, f32[1,1,1024]{2,1,0:T(1,128)}, u32[]{:S(2)}) copy-start(f32[1,1,1024]{2,1,0:T(1,128)} %get-tuple-element.49) | copy-start | bytes 12292
  359.6 13.2 %copy-start.65 = (f32[1,1,1024]{2,1,0:T(1,128)S(1)}, f32[1,1,1024]{2,1,0:T(1,128)}, u32[]{:S(2)}) copy-start(f32[1,1,1024]{2,1,0:T(1,128)} %get-tuple-element.50) | copy-start | bytes 12292
  359.6 13.2 %copy-start.66 = (f32[1,1,1024]{2,1,0:T(1,128)S(1)}, f32[1,1,1024]{2,1,0:T(1,128)}, u32[]{:S(2)}) copy-start(f32[1,1,1024]{2,1,0:T(1,128)} %get-tuple-element.51) | copy-start | bytes 12292
  359.6 13.2 %copy-start.67 = (f32[1,1,1024]{2,1,0:T(1,128)S(1)}, f32[1,1,1024]{2,1,0:T(1,128)}, u32[]{:S(2)}) copy-start(f32[1,1,1024]{2,1,0:T(1,128)} %get-tuple-element.52) | copy-start | bytes 12292
  359.6 13.2 %copy-start.68 = (f32[1,1,1024]{2,1,0:T(1,128)S(1)}, f32[1,1,1024]{2,1,0:T(1,128)}, u32[]{:S(2)}) copy-start(f32[1,1,1024]{2,1,0:T(1,128)} %get-tuple-element.53) | copy-start | bytes 12292
  359.6 13.2 %copy-start.69 = (f32[1,1,1024]{2,1,0:T(1,128)S(1)}, f32[1,1,1024]{2,1,0:T(1,128)}, u32[]{:S(2)}) copy-start(f32[1,1,1024]{2,1,0:T(1,128)} %get-tuple-element.54) | copy-start | bytes 12292
  359.6 13.2 %copy-start.70 = (f32[1,1,1024]{2,1,0:T(1,128)S(1)}, f32[1,1,1024]{2,1,0:T(1,128)}, u32[]{:S(2)}) copy-start(f32[1,1,1024]{2,1,0:T(1,128)} %get-tuple-element.55) | copy-start | bytes 12292
  359.6 13.2 %copy-start.71 = (f32[1,1,1024]{2,1,0:T(1,128)S(1)}, f32[1,1,1024]{2,1,0:T(1,128)}, u32[]{:S(2)}) copy-start(f32[1,1,1024]{2,1,0:T(1,128)} %get-tuple-element.56) | copy-start | bytes 12292
  359.6 13.2 %copy-start.72 = (f32[1,1,1024]{2,1,0:T(1,128)S(1)}, f32[1,1,1024]{2,1,0:T(1,128)}, u32[]{:S(2)}) copy-start(f32[1,1,1024]{2,1,0:T(1,128)} %get-tuple-element.57) | copy-start | bytes 12292
  359.7 13.2 %copy-start.73 = (f32[1,1,1024]{2,1,0:T(1,128)S(1)}, f32[1,1,1024]{2,1,0:T(1,128)}, u32[]{:S(2)}) copy-start(f32[1,1,1024]{2,1,0:T(1,128)} %get-tuple-element.58) | copy-start | bytes 12292
  359.7 13.2 %copy-start.74 = (f32[1,1,1024]{2,1,0:T(1,128)S(1)}, f32[1,1,1024]{2,1,0:T(1,128)}, u32[]{:S(2)}) copy-start(f32[1,1,1024]{2,1,0:T(1,128)} %get-tuple-element.59) | copy-start | bytes 12292
  359.7 13.2 %copy-start.75 = (f32[1,1,1024]{2,1,0:T(1,128)S(1)}, f32[1,1,1024]{2,1,0:T(1,128)}, u32[]{:S(2)}) copy-start(f32[1,1,1024]{2,1,0:T(1,128)} %get-tuple-element.60) | copy-start | bytes 12292
  359.7 13.2 %copy-start.76 = (f32[1,1,1024]{2,1,0:T(1,128)S(1)}, f32[1,1,1024]{2,1,0:T(1,128)}, u32[]{:S(2)}) copy-start(f32[1,1,1024]{2,1,0:T(1,128)} %get-tuple-element.61) | copy-start | bytes 12292
  359.7 13.2 %copy-start.77 = (f32[1,1,1024]{2,1,0:T(1,128)S(1)}, f32[1,1,1024]{2,1,0:T(1,128)}, u32[]{:S(2)}) copy-start(f32[1,1,1024]{2,1,0:T(1,128)} %get-tuple-element.62) | copy-start | bytes 12292
  359.7 13.2 %copy-start.78 = (f32[1,1,1024]{2,1,0:T(1,128)S(1)}, f32[1,1,1024]{2,1,0:T(1,128)}, u32[]{:S(2)}) copy-start(f32[1,1,1024]{2,1,0:T(1,128)} %get-tuple-element.63) | copy-start | bytes 12292
  359.7 13.2 %copy-start.79 = (f32[1,1,1024]{2,1,0:T(1,128)S(1)}, f32[1,1,1024]{2,1,0:T(1,128)}, u32[]{:S(2)}) copy-start(f32[1,1,1024]{2,1,0:T(1,128)} %get-tuple-element.64) | copy-start | bytes 12292
  359.7 13.2 %copy-start.80 = (f32[1,1,1024]{2,1,0:T(1,128)S(1)}, f32[1,1,1024]{2,1,0:T(1,128)}, u32[]{:S(2)}) copy-start(f32[1,1,1024]{2,1,0:T(1,128)} %get-tuple-element.65) | copy-start | bytes 12292
  359.7 13.2 %copy-start.81 = (f32[1,1,1024]{2,1,0:T(1,128)S(1)}, f32[1,1,1024]{2,1,0:T(1,128)}, u32[]{:S(2)}) copy-start(f32[1,1,1024]{2,1,0:T(1,128)} %get-tuple-element.66) | copy-start | bytes 12292
  359.7 13.2 %copy-start.82 = (f32[1,1,1024]{2,1,0:T(1,128)S(1)}, f32[1,1,1024]{2,1,0:T(1,128)}, u32[]{:S(2)}) copy-start(f32[1,1,1024]{2,1,0:T(1,128)} %get-tuple-element.67) | copy-start | bytes 12292
  359.8 13.2 %copy-start.83 = (f32[1,1,1024]{2,1,0:T(1,128)S(1)}, f32[1,1,1024]{2,1,0:T(1,128)}, u32[]{:S(2)}) copy-start(f32[1,1,1024]{2,1,0:T(1,128)} %get-tuple-element.30) | copy-start | bytes 12292
  359.8 13.2 %copy-start.84 = (f32[1,1,1024]{2,1,0:T(1,128)S(1)}, f32[1,1,1024]{2,1,0:T(1,128)}, u32[]{:S(2)}) copy-start(f32[1,1,1024]{2,1,0:T(1,128)} %get-tuple-element.31) | copy-start | bytes 12292
  359.8 13.2 %copy-start.85 = (f32[1,1,1024]{2,1,0:T(1,128)S(1)}, f32[1,1,1024]{2,1,0:T(1,128)}, u32[]{:S(2)}) copy-start(f32[1,1,1024]{2,1,0:T(1,128)} %get-tuple-element.32) | copy-start | bytes 12292
  359.8 13.2 %copy-start.86 = (f32[1,1,1024]{2,1,0:T(1,128)S(1)}, f32[1,1,1024]{2,1,0:T(1,128)}, u32[]{:S(2)}) copy-start(f32[1,1,1024]{2,1,0:T(1,128)} %get-tuple-element.33) | copy-start | bytes 12292
  359.8 13.2 %copy-start.87 = (f32[1,1,1024]{2,1,0:T(1,128)S(1)}, f32[1,1,1024]{2,1,0:T(1,128)}, u32[]{:S(2)}) copy-start(f32[1,1,1024]{2,1,0:T(1,128)} %get-tuple-element.34) | copy-start | bytes 12292
  359.8 13.2 %copy-start.88 = (f32[1,1,1024]{2,1,0:T(1,128)S(1)}, f32[1,1,1024]{2,1,0:T(1,128)}, u32[]{:S(2)}) copy-start(f32[1,1,1024]{2,1,0:T(1,128)} %get-tuple-element.35) | copy-start | bytes 12292
  359.8 12.6 %collective-permute-start.3 = (bf16[2,127,1024]{2,1,0:T(8,128)(2,1)S(1)}, bf16[2,127,1024]{2,1,0:T(8,128)(2,1)S(1)}, u32[]{:S(2)}, u32[]{:S(2)}) collective-permute-start(bf16[2,127,1024]{2,1,0:T(8,128)(2,1)S(1)} %slice.2294), channel_id=1, source_target_pairs={{0,4},{4,8},{8,12},{12,16},{16,20},{20,24},{24,28},{28,32},{32,36}... | collective-permute-start | bytes 1560584 | tf_op jit(solution)/shard_map/ppermute | solution.py:372
  408.7 32.3 %copy-start.7 = (bf16[272,1024]{1,0:T(8,128)(2,1)S(1)}, bf16[272,1024]{1,0:T(8,128)(2,1)}, u32[]{:S(2)}) copy-start(bf16[272,1024]{1,0:T(8,128)(2,1)} %copy-done.6) | copy-start | bytes 1671172
  408.7 32.3 %copy-start.11 = (bf16[272,1024]{1,0:T(8,128)(2,1)S(1)}, bf16[272,1024]{1,0:T(8,128)(2,1)}, u32[]{:S(2)}) copy-start(bf16[272,1024]{1,0:T(8,128)(2,1)} %copy-done.10) | copy-start | bytes 1671172
  (52 other events, 276.2 us)
Sparse Core Ops, SparseCore 0:
  244.2 30.8 reduce-scatter.2
  296.2 34.5 all-gather.1
  408.8 32.1 reduce-scatter.4

commit v2 on v1

v2 whole, which is shorter than its diff:
```python
import functools

import jax
import jax.numpy as jnp
from jax import lax
from jax.experimental import pallas as pl
from jax.experimental.pallas import tpu as pltpu
from jax.sharding import PartitionSpec as P

EPS = 1e-06
MESH = pl.DeviceIdType.MESH
RING = 8
VMEM = pl.BlockSpec(memory_space=pltpu.VMEM)
HBM = pl.BlockSpec(memory_space=pltpu.HBM)


def place():
    seq = lax.axis_index("seq")
    return seq // (2 * RING), (seq // 2) % RING, seq % 2


def seq_of(y, z, core):
    return (y * RING + z) * 2 + core


class Gather:
    MOVES = (
        ("a1", "up", True, 0, None),
        ("b1", "down", True, 0, None),
        ("c1", "y", True, 0, None),
        ("a2", "up", True, -1, None),
        ("b2", "down", True, 1, None),
        ("a3", "up", True, -2, None),
        ("b3", "down", True, 2, None),
        ("c2", "y", True, -2, 1),
        ("c3", "y", True, 2, 0),
        ("a4", "up", True, -3, 0),
        ("b4", "down", True, 3, 1),
        ("a5", "up", False, 0, None),
        ("b5", "down", False, 0, None),
        ("c4", "y", True, -3, None),
        ("c5", "y", True, 3, None),
        ("a6", "up", False, -1, 0),
        ("b6", "down", False, 1, 1),
        ("c6", "y", True, 4, 0),
        ("c7", "y", True, 4, 1),
    )
    COUNT = len(MOVES)

    def __init__(self, slot, own, send, recv, side_send, side_recv):
        self.y, self.z, self.core = place()
        self.slot, self.own = slot, own
        self.send, self.recv = send, recv
        self.side_send, self.side_recv = side_send, side_recv
        self.index = {move[0]: at for at, move in enumerate(self.MOVES)}
        self.pending = []

    def target(self, direction):
        if direction == "up":
            return seq_of(self.y, (self.z + 1) % RING, self.core)
        if direction == "down":
            return seq_of(self.y, (self.z + RING - 1) % RING, self.core)
        return seq_of(1 - self.y, self.z, self.core)

    def block(self, same, dz, core=None):
        y = self.y if same else 1 - self.y
        return seq_of(y, (self.z + dz + RING) % RING, self.core if core is None else core)

    def copy(self, name):
        at = self.index[name]
        _, direction, same, dz, half = self.MOVES[at]
        block = self.block(same, dz)
        dst = self.slot(block, half)
        src = self.own if same and dz == 0 else dst
        return pltpu.make_async_remote_copy(
            src_ref=src,
            dst_ref=dst,
            send_sem=self.send.at[at],
            recv_sem=self.recv.at[at],
            device_id={"seq": self.target(direction)},
            device_id_type=MESH,
        )

    def start(self, *names):
        for name in names:
            self.copy(name).start()

    def landed(self, name):
        at = self.index[name]
        _, direction, same, dz, half = self.MOVES[at]
        if direction == "y":
            block = self.block(not same, dz)
        else:
            block = self.block(same, dz + (-1 if direction == "up" else 1))
        got = self.slot(block, half)
        pltpu.make_async_copy(got, got, self.recv.at[at]).wait()
        side = pltpu.make_async_remote_copy(
            src_ref=got,
            dst_ref=got,
            send_sem=self.side_send.at[at],
            recv_sem=self.side_recv.at[at],
            device_id={"seq": seq_of(self.y, self.z, 1 - self.core)},
            device_id_type=MESH,
        )
        side.start()

    def side_own(self):
        return pltpu.make_async_remote_copy(
            src_ref=self.own,
            dst_ref=self.slot(self.block(True, 0), None),
            send_sem=self.side_send.at[self.COUNT],
            recv_sem=self.side_recv.at[self.COUNT],
            device_id={"seq": seq_of(self.y, self.z, 1 - self.core)},
            device_id_type=MESH,
        )

    def run(self, local_sem):
        keep = pltpu.make_async_copy(self.own, self.slot(self.block(True, 0), None), local_sem)
        self.start("a1", "b1", "c1")
        self.side_own().start()
        keep.start()
        self.landed("a1")
        self.start("a2")
        self.landed("b1")
        self.start("b2")
        self.landed("c1")
        self.landed("a2")
        self.start("a3", "c2")
        self.landed("b2")
        self.start("b3", "c3")
        self.start("a5", "b5")
        self.landed("a3")
        self.start("a4", "c4")
        self.landed("b3")
        self.start("b4", "c5")
        self.landed("a5")
        self.start("a6")
        self.landed("b5")
        self.start("b6")
        self.landed("a4")
        self.start("c6")
        self.landed("b4")
        self.start("c7")
        for name in ("c2", "c3", "a6", "b6", "c4", "c5", "c6", "c7"):
            self.landed(name)
        keep.wait()
        for at, (name, direction, same, dz, half) in enumerate(self.MOVES):
            self.copy(name).wait_send()
            if direction == "y":
                block = (not same, dz)
            else:
                block = (same, dz + (-1 if direction == "up" else 1))
            mine = self.slot(self.block(*block), half)
            pltpu.make_async_copy(mine, mine, self.side_send.at[at]).wait()
            other = self.slot(self.block(*block, 1 - self.core), half)
            pltpu.make_async_copy(other, other, self.side_recv.at[at]).wait()
        side = self.side_own()
        side.wait_send()
        other = self.slot(self.block(True, 0, 1 - self.core), None)
        pltpu.make_async_copy(other, other, self.side_recv.at[self.COUNT]).wait()


def mixer_kernel(
    ids, tail, shard, table, gain, se, mr, weight_hbm, out,
    w, weight, tail_all, part, ids_all, sf, gf, query, mixf, mixed, send_buf, recv_buf, own_part, base, xs, xn,
    rim_send, rim_recv, far_send, far_recv,
    send, recv, side_send, side_recv, a2a_send, a2a_recv, x_send, x_recv,
    rs_send, rs_recv, ag_send, ag_recv, relay_send, relay_recv, halo_send, halo_recv, local,
):
    section = lax.axis_index("section")
    tensor = lax.axis_index("tensor")
    seq = lax.axis_index("seq")
    y, z, core = place()
    count, share, depth = tail.shape
    vocab, width = table.shape
    wide = share // 3
    half = vocab // 2
    ways = w.shape[0]
    micro = gf.shape[0]
    tiles = gf.shape[1]
    length = gf.shape[2] // 2
    taps = mr.shape[0]
    short_taps = se.shape[1]
    lane = 128
    block = 256
    chunks = ((0, 128), (128, micro * length - 128))
    ahead = (tensor + 1 + core * (ways - 2)) % ways
    behind = (tensor + ways - 1 - core * (ways - 2)) % ways
    far = (tensor + 2) % ways
    barrier = pltpu.get_barrier_semaphore()

    def greet(**axes):
        pl.semaphore_signal(barrier, inc=1, device_id=axes, device_id_type=MESH)

    def remote(src, dst, send_sem, recv_sem, **axes):
        return pltpu.make_async_remote_copy(
            src_ref=src, dst_ref=dst, send_sem=send_sem, recv_sem=recv_sem,
            device_id=axes, device_id_type=MESH,
        )

    def arrival(ref, sem):
        pltpu.make_async_copy(ref, ref, sem).wait()

    def lanes(tile):
        return pl.ds(pl.multiple_of(tile * lane, lane), lane)

    def short(tile, stream, start, rows):
        total = jnp.zeros((rows, lane), jnp.float32)
        for tap in range(short_taps):
            total += se[stream, tap : tap + 1, lanes(tile)] * sf[
                stream, tile, start - tap : start - tap + rows, :
            ]
        return total

    def gate(mb, tile, start, rows, at):
        values = short(tile, 1, start, rows) * short(tile, 2, start, rows)
        gf[mb, tile, at : at + rows, :] = values.astype(jnp.bfloat16).astype(jnp.float32)

    def medium(mb):
        def one_tile(tile, carry):
            total = jnp.zeros((length, lane), jnp.float32)
            reach = length + taps - 8
            for shift in range(8):
                begin = length - (taps - 8) - shift
                window = gf[mb, tile, begin : begin + reach, :]
                for step in range(taps // 8):
                    tap = 8 * step + shift
                    at = taps - 8 - 8 * step
                    total += mr[tap : tap + 1, lanes(tile)] * window[at : at + length]
            mixf[mb * length : (mb + 1) * length, lanes(tile)] = query[mb, tile] * total
            return carry

        lax.fori_loop(0, tiles, one_tile, 0)

    def partial_to(chunk, owner, finish):
        first, rows = chunks[chunk]
        window = slice(first, first + rows)

        def one_block(at, carry):
            inner = pl.ds(pl.multiple_of(at * block, block), block)
            outer = pl.ds(pl.multiple_of(owner * width + at * block, block), block)
            term = jnp.dot(mixed[window], weight[:, outer], preferred_element_type=jnp.float32)
            finish(window, inner, term)
            return carry

        lax.fori_loop(0, width // block, one_block, 0)

    def hop(chunk, at, to):
        first, rows = chunks[chunk]
        window = slice(first, first + rows)
        return remote(
            send_buf.at[at, window], recv_buf.at[at, window],
            rs_send.at[chunk * 3 + at], rs_recv.at[chunk * 3 + at], tensor=to,
        )

    def fill(at):
        def finish(window, inner, term):
            send_buf[at, window, inner] = term.astype(jnp.bfloat16)

        return finish

    def reduce_start(chunk):
        first, rows = chunks[chunk]
        window = slice(first, first + rows)
        mixed[window] = mixf[window].astype(jnp.bfloat16)
        partial_to(chunk, far, fill(0))
        hop(chunk, 0, ahead).start()
        partial_to(chunk, behind, fill(2))
        hop(chunk, 2, behind).start()

    def reduce_middle(chunk):
        hop(chunk, 0, ahead).wait_recv()

        def finish(window, inner, term):
            both = term + recv_buf[0, window, inner].astype(jnp.float32)
            send_buf[1, window, inner] = both.astype(jnp.bfloat16)

        partial_to(chunk, ahead, finish)
        hop(chunk, 1, ahead).start()

        def keep(window, inner, term):
            own_part[window, inner] = term

        partial_to(chunk, tensor, keep)

    def reduce_end(chunk):
        first, rows = chunks[chunk]
        hop(chunk, 2, behind).wait_recv()
        hop(chunk, 1, ahead).wait_recv()
        lines = 16

        def add(at, carry):
            window = pl.ds(pl.multiple_of(first + at * lines, lines), lines)
            total = own_part[window] + recv_buf[1, window].astype(jnp.float32)
            total += recv_buf[2, window].astype(jnp.float32)
            out[window] = (base[window] + total).astype(jnp.bfloat16)
            return carry

        lax.fori_loop(0, rows // lines, add, 0)

    def reduce_close():
        for chunk in range(2):
            hop(chunk, 0, ahead).wait_send()
            hop(chunk, 1, ahead).wait_send()
            hop(chunk, 2, behind).wait_send()

    def relay(chunk):
        first, rows = chunks[chunk]
        window = slice(first, first + rows)
        return remote(
            out.at[window], xs.at[tensor, window],
            relay_send.at[chunk], relay_recv.at[chunk], section=1,
        )

    load_weight = pltpu.make_async_copy(weight_hbm, weight, local.at[2])

    @pl.when(section == 0)
    def _():
        greet(tensor=ahead)
        greet(tensor=behind)

        def greet_seq(step, carry):
            greet(seq=(seq + step) % count)
            return carry

        lax.fori_loop(1, count, greet_seq, 0)
        pl.semaphore_wait(barrier, count + 2)
        load_weight.start()

        ids_on = remote(
            ids, ids_all.at[:, 0:length], halo_send.at[0], halo_recv.at[0],
            seq=(seq + 1) % count,
        )

        @pl.when(seq < count - 1)
        def _():
            ids_on.start()

        @pl.when(seq == 0)
        def _():
            ids_all[:, 0:length] = jnp.full((micro, length, lane), -1, jnp.int32)

        rows = pl.ds(pl.multiple_of(core * half, half), half)

        def along(at, src, owner, to):
            return remote(src, w.at[owner, rows, 0:width], x_send.at[at], x_recv.at[at], tensor=to)

        def across(at, owner):
            piece = w.at[owner, rows, 0:width]
            return remote(
                piece, piece, x_send.at[at], x_recv.at[at], seq=seq_of(y, z, 1 - core)
            )

        mine = table.at[rows]
        along(0, mine, tensor, ahead).start()
        along(1, mine, tensor, behind).start()
        keep = pltpu.make_async_copy(table, w.at[tensor, 0:vocab, 0:width], local.at[0])
        keep.start()

        def spread(step):
            to = (seq + step) % count
            return remote(
                tail.at[to],
                tail_all.at[:, pl.ds(pl.multiple_of(seq * depth, depth), depth)],
                a2a_send.at[step], a2a_recv.at[step], seq=to,
            )

        def spread_start(step, carry):
            spread(step).start()
            return carry

        lax.fori_loop(1, count, spread_start, 0)
        keep_tail = pltpu.make_async_copy(
            tail.at[seq],
            tail_all.at[:, pl.ds(pl.multiple_of(seq * depth, depth), depth)],
            local.at[1],
        )
        keep_tail.start()
        ids_all[:, length : 2 * length] = ids[...]

        along(0, mine, tensor, ahead).wait_recv()
        along(2, w.at[behind, rows, 0:width], behind, ahead).start()
        across(3, behind).start()
        along(1, mine, tensor, behind).wait_recv()
        across(4, ahead).start()
        got = w.at[far, rows, 0:width]
        arrival(got, x_recv.at[2])
        across(5, far).start()
        keep.wait()
        for at, owner in ((3, behind), (4, ahead), (5, far)):
            across(at, owner).wait_recv()
        along(0, mine, tensor, ahead).wait_send()
        along(1, mine, tensor, behind).wait_send()
        arrival(got, x_send.at[2])
        for at, owner in ((3, behind), (4, ahead), (5, far)):
            across(at, owner).wait_send()

        lines = 32

        def normalise(at, carry):
            window = pl.ds(pl.multiple_of(at * lines, lines), lines)
            total = jnp.zeros((lines, 1), jnp.float32)
            for way in range(ways):
                values = w[way, window, 0:width].astype(jnp.float32)
                total += jnp.sum(values * values, axis=1, keepdims=True)
            scale = lax.rsqrt(total / (ways * width) + EPS)
            for way in range(ways):
                values = w[way, window, 0:width].astype(jnp.float32)
                values = values * scale * gain[:, way * width : (way + 1) * width]
                w[way, window, 0:width] = values.astype(jnp.bfloat16)
            return carry

        lax.fori_loop(0, vocab // lines, normalise, 0)

        def spread_wait(step, carry):
            spread(step).wait_send()
            arrival(tail_all.at[:, pl.ds(0, depth)], a2a_recv.at[step])
            return carry

        lax.fori_loop(1, count, spread_wait, 0)
        keep_tail.wait()
        total = jnp.zeros((share, vocab), jnp.float32)
        for way in range(ways):
            total += lax.dot_general(
                tail_all[:, way * width : (way + 1) * width],
                w[way, 0:vocab, 0:width],
                (((1,), (1,)), ((), ())),
                preferred_element_type=jnp.float32,
            )
        for stream in range(3):
            part[stream] = total[stream * wide : (stream + 1) * wide].astype(jnp.bfloat16)

        def slot(owner, part_of):
            at, some = owner * wide, wide
            if part_of is not None:
                some = wide // 2
                at = at + part_of * some
            return w.at[0:3, pl.ds(pl.multiple_of(at, some), some), width : width + vocab]

        Gather(slot, part, send, recv, side_send, side_recv).run(local.at[0])
        load_weight.wait()

        @pl.when(seq > 0)
        def _():
            ids_on.wait_recv()

        onehot = w.at[3, 0 : 2 * length, width : width + vocab]

        def streams(mb):
            for part_at in range(vocab // lane):
                number = lax.broadcasted_iota(jnp.int32, (2 * length, lane), 1) + part_at * lane
                hit = jnp.where(ids_all[mb] == number, 1.0, 0.0).astype(jnp.bfloat16)
                w[3, 0 : 2 * length, width + part_at * lane : width + (part_at + 1) * lane] = hit

            def one_block(at, carry):
                stream, inner = at // (width // block), at % (width // block)
                columns = pl.ds(pl.multiple_of(inner * block, block), block)
                values = lax.dot_general(
                    onehot[...],
                    w[stream, columns, width : width + vocab],
                    (((1,), (1,)), ((), ())),
                    preferred_element_type=jnp.float32,
                ).astype(jnp.bfloat16).astype(jnp.float32)
                for side in range(block // lane):
                    sf[stream, inner * (block // lane) + side, 8 : 8 + 2 * length, :] = values[
                        :, side * lane : (side + 1) * lane
                    ]
                return carry

            lax.fori_loop(0, 3 * width // block, one_block, 0)

            def own_rows(at, carry):
                columns = pl.ds(pl.multiple_of(at * block, block), block)
                values = jnp.dot(
                    onehot[...], table[:, columns], preferred_element_type=jnp.float32
                )
                base[mb * length : (mb + 1) * length, columns] = values[length : 2 * length]
                return carry

            lax.fori_loop(0, width // block, own_rows, 0)

            def one_tile(tile, carry):
                query[mb, tile] = short(tile, 0, 8 + length, length)
                gate(mb, tile, 8, length, 0)
                gate(mb, tile, 8 + length, length, length)
                return carry

            lax.fori_loop(0, tiles, one_tile, 0)

        sf[:, :, 0:8, :] = jnp.zeros((3, tiles, 8, lane), jnp.float32)
        streams(0)
        medium(0)
        reduce_start(0)
        streams(1)
        reduce_middle(0)
        medium(1)
        reduce_end(0)
        relay(0).start()
        reduce_start(1)
        reduce_middle(1)
        reduce_end(1)
        relay(1).start()
        reduce_close()
        relay(0).wait_send()
        relay(1).wait_send()

        @pl.when(seq < count - 1)
        def _():
            ids_on.wait_send()

    @pl.when(section == 1)
    def _():
        greet(seq=seq_of(y, (z + 1) % RING, core))
        greet(seq=seq_of(y, (z + RING - 1) % RING, core))
        greet(seq=seq_of(1 - y, z, core))
        greet(seq=seq_of(y, z, 1 - core))
        greet(tensor=ahead)
        greet(tensor=behind)
        greet(section=0)

        @pl.when(seq > 0)
        def _():
            greet(seq=(seq + count - 1) % count)

        @pl.when(seq < count - 1)
        def _():
            pl.semaphore_wait(barrier, 7)

        @pl.when(seq == count - 1)
        def _():
            pl.semaphore_wait(barrier, 6)

        load_weight.start()
        per = width // depth

        def slot(owner, part_of):
            at, some = (owner % per) * depth, depth
            if part_of is not None:
                some = depth // 2
                at = at + part_of * some
            return w.at[owner // per, pl.ds(pl.multiple_of(at, some), some)]

        Gather(slot, shard, send, recv, side_send, side_recv).run(local.at[0])
        load_weight.wait()

        def share_out(chunk, at, owner, to):
            first, rows = chunks[chunk]
            piece = xs.at[owner, first : first + rows]
            return remote(
                piece, piece, ag_send.at[chunk * 3 + at], ag_recv.at[chunk * 3 + at], tensor=to
            )

        def gather_start(chunk):
            first, rows = chunks[chunk]
            arrival(xs.at[tensor, first : first + rows], relay_recv.at[chunk])
            share_out(chunk, 0, tensor, ahead).start()
            share_out(chunk, 1, tensor, behind).start()

        def gather_middle(chunk):
            first, rows = chunks[chunk]
            arrival(xs.at[behind, first : first + rows], ag_recv.at[chunk * 3])
            share_out(chunk, 2, behind, ahead).start()

        def gather_end(chunk):
            first, rows = chunks[chunk]
            arrival(xs.at[ahead, first : first + rows], ag_recv.at[chunk * 3 + 1])
            arrival(xs.at[far, first : first + rows], ag_recv.at[chunk * 3 + 2])

        def gather_close():
            for chunk in range(2):
                share_out(chunk, 0, tensor, ahead).wait_send()
                share_out(chunk, 1, tensor, behind).wait_send()
                share_out(chunk, 2, behind, ahead).wait_send()

        def project(chunk):
            first, rows = chunks[chunk]
            lines = 16

            def normalise(at, carry):
                window = pl.ds(pl.multiple_of(first + at * lines, lines), lines)
                total = jnp.zeros((lines, 1), jnp.float32)
                for way in range(ways):
                    values = xs[way, window].astype(jnp.float32)
                    total += jnp.sum(values * values, axis=1, keepdims=True)
                scale = lax.rsqrt(total / (ways * width) + EPS)
                for way in range(ways):
                    values = xs[way, window].astype(jnp.float32)
                    values = values * scale * gain[:, way * width : (way + 1) * width]
                    xn[way, window] = values.astype(jnp.bfloat16)
                base[window] = xs[tensor, window].astype(jnp.float32)
                return carry

            lax.fori_loop(0, rows // lines, normalise, 0)

            def one_block(at, carry):
                stream, inner = at // (width // block), at % (width // block)
                columns = pl.ds(pl.multiple_of(at * block, block), block)
                total = jnp.zeros((rows, block), jnp.float32)
                for way in range(ways):
                    total += jnp.dot(
                        xn[way, first : first + rows],
                        w[way, :, columns],
                        preferred_element_type=jnp.float32,
                    )
                total = total.astype(jnp.bfloat16).astype(jnp.float32)
                for side in range(block // lane):
                    tile = inner * (block // lane) + side
                    piece = total[:, side * lane : (side + 1) * lane]
                    for mb in range(micro):
                        begin = max(first, mb * length)
                        end = min(first + rows, (mb + 1) * length)
                        if begin < end:
                            to = mb * (length + 8) + 8 + begin - mb * length
                            sf[stream, tile, to : to + end - begin, :] = piece[
                                begin - first : end - first
                            ]
                return carry

            lax.fori_loop(0, 3 * width // block, one_block, 0)

        def rim(mb):
            return remote(
                rim_send.at[mb], rim_recv.at[mb], halo_send.at[mb], halo_recv.at[mb],
                seq=(seq + 1) % count,
            )

        def gated_rim(mb):
            return remote(
                far_send.at[mb], far_recv.at[mb], halo_send.at[micro + mb], halo_recv.at[micro + mb],
                seq=(seq + 1) % count,
            )

        def rim_start(mb):
            last = (mb + 1) * (length + 8)
            rim_send[mb] = sf[:, :, last - 16 : last, :].astype(jnp.bfloat16)

            @pl.when(seq < count - 1)
            def _():
                rim(mb).start()

        def shorts(mb):
            first = mb * (length + 8)

            @pl.when(seq > 0)
            def _():
                rim(mb).wait_recv()
                sf[:, :, first : first + 8, :] = rim_recv[mb].astype(jnp.float32)[:, :, 8:16]

            @pl.when(seq == 0)
            def _():
                sf[:, :, first : first + 8, :] = jnp.zeros((3, tiles, 8, lane), jnp.float32)

            def one_tile(tile, carry):
                query[mb, tile] = short(tile, 0, first + 8, length)
                gate(mb, tile, first + 8, length, length)
                far_send[mb, tile] = gf[mb, tile, 2 * length - taps : 2 * length, :].astype(
                    jnp.bfloat16
                )
                return carry

            lax.fori_loop(0, tiles, one_tile, 0)

            @pl.when(seq < count - 1)
            def _():
                gated_rim(mb).start()

        def gated_end(mb):
            @pl.when(seq > 0)
            def _():
                gated_rim(mb).wait_recv()

                def one_tile(tile, carry):
                    gf[mb, tile, length - taps : length, :] = far_recv[mb, tile].astype(
                        jnp.float32
                    )
                    return carry

                lax.fori_loop(0, tiles, one_tile, 0)

            @pl.when(seq == 0)
            def _():
                gf[mb, :, 0:length, :] = jnp.zeros((tiles, length, lane), jnp.float32)

        gather_start(0)
        gather_middle(0)
        gather_end(0)
        gather_start(1)
        project(0)
        gather_middle(1)
        gather_end(1)
        project(1)
        rim_start(0)
        rim_start(1)
        shorts(0)
        shorts(1)
        gated_end(0)
        medium(0)
        reduce_start(0)
        gated_end(1)
        reduce_middle(0)
        medium(1)
        reduce_end(0)
        reduce_start(1)
        reduce_middle(1)
        reduce_end(1)
        reduce_close()
        gather_close()

        @pl.when(seq < count - 1)
        def _():
            for mb in range(micro):
                rim(mb).wait_send()
                gated_rim(mb).wait_send()


def body(token_ids, embed_table, norm_gain, in_weight, se_filter, mr_filter, out_weight):
    micro, length = token_ids.shape
    vocab, width = embed_table.shape
    full = norm_gain.shape[1]
    count = lax.axis_size("seq")
    ways = full // width
    lane = 128
    tiles = width // lane
    rows = micro * length
    taps = mr_filter.shape[1]
    depth = in_weight.shape[1]
    share = 3 * width // count
    shard = in_weight[0].reshape(depth, 3 * width)
    tail = in_weight[0].reshape(depth, 3, count, width // count).transpose(2, 1, 3, 0)
    tail = tail.reshape(count, share, depth)
    ids = jnp.broadcast_to(token_ids[:, :, None], (micro, length, lane))
    moves = Gather.COUNT
    bf16, f32 = jnp.bfloat16, jnp.float32
    scratch, dma = pltpu.VMEM, pltpu.SemaphoreType.DMA
    result = pl.pallas_call(
        mixer_kernel,
        out_shape=jax.ShapeDtypeStruct((rows, width), bf16),
        in_specs=[VMEM, HBM, HBM, VMEM, VMEM, VMEM, VMEM, HBM],
        out_specs=VMEM,
        scratch_shapes=[
            scratch((ways, width, 3 * width), bf16),
            scratch((width, full), bf16),
            scratch((share, full), bf16),
            scratch((3, share // 3, vocab), bf16),
            scratch((micro, 2 * length, lane), jnp.int32),
            scratch((3, tiles, 2 * length + 16, lane), f32),
            scratch((micro, tiles, 2 * length, lane), f32),
            scratch((micro, tiles, length, lane), f32),
            scratch((rows, width), f32),
            scratch((rows, width), bf16),
            scratch((3, rows, width), bf16),
            scratch((3, rows, width), bf16),
            scratch((rows, width), f32),
            scratch((rows, width), f32),
            scratch((ways, rows, width), bf16),
            scratch((ways, rows, width), bf16),
            scratch((micro, 3, tiles, 16, lane), bf16),
            scratch((micro, 3, tiles, 16, lane), bf16),
            scratch((micro, tiles, taps, lane), bf16),
            scratch((micro, tiles, taps, lane), bf16),
            dma((moves,)),
            dma((moves,)),
            dma((moves + 1,)),
            dma((moves + 1,)),
            dma((count,)),
            dma((count,)),
            dma((6,)),
            dma((6,)),
            dma((6,)),
            dma((6,)),
            dma((6,)),
            dma((6,)),
            dma((2,)),
            dma((2,)),
            dma((2 * micro,)),
            dma((2 * micro,)),
            dma((3,)),
        ],
        compiler_params=pltpu.CompilerParams(
            collective_id=0, has_side_effects=True, vmem_limit_bytes=60 << 20
        ),
        name="mixer",
    )(ids, tail, shard, embed_table, norm_gain, se_filter[0], mr_filter[0], out_weight[0])
    return result.reshape(1, micro, length, width)


def solution(mesh):
    in_specs = (
        P(None, "seq"),
        P(None, "tensor"),
        P("section", None),
        P("section", "seq", None, "tensor"),
        P("section", None, None, "tensor"),
        P("section", None, "tensor"),
        P("section", "tensor", None),
    )
    out_specs = P("section", None, "seq", "tensor")
    return jax.shard_map(body, mesh=mesh, in_specs=in_specs, out_specs=out_specs, check_vma=False)
```

time: 459 us -> 208 us (0.45); the launches traced: 450 us -> 208 us
  waiting for transfers between devices: 123 us -> 0 us
  other arithmetic: 85 us -> 0 us
  Pallas kernels: 117 us -> 199 us
  local copies, waits for them, and re-layouts: 67.1 us -> 8.5 us
  matrix products: 34.1 us -> 0 us
  between operations: 14.9 us -> 0.02 us
  starting transfers between devices: 8.76 us -> 0 us
    pallas_call x1, Pallas kernels: 117 us -> 199 us  [body(): pl.pallas_call(mixer_kernel, out_shape=jax.ShapeDtypeStruct((rows, width)...]
    convert_element_type x7 -> x0, other arithmetic: 75.6 us -> none  [the longest x2 60 us: finish(): mixed = (query * medium).astype(jnp.bfloat16).reshape(micro * length, width)]
    reduce_scatter x2 -> x0, waiting for transfers between devices: 63 us -> none  [finish(): lax.psum_scatter(terms.astype(jnp.bfloat16), 'tensor', scatter_dimension=...]
    all_gather x1 -> x0, waiting for transfers between devices: 34.5 us -> none  [body(): normed = normalised(lax.all_gather(arrived, 'tensor', axis=1, tiled=True))]
    dot_general x5 -> x0, matrix products: 34.1 us -> none  [the longest x2 14.4 us: finish(): terms = jnp.dot(mixed, weight, preferred_element_type=jnp.float32)]
    slice x15 -> x0, local copies, waits for them, and re-layouts: 31.9 us -> none  [the longest x10 15.1 us: causal_sum(): total = total + coeffs[tap][None, None] * extended[:, begin:begin + length]]
    ppermute x4 -> x0, waiting for transfers between devices: 25.6 us -> none  [passed_along(): lax.ppermute(value, axis, [(source, source + steps) for source in range(i...]
    unnamed x195 -> x3, local copies, waits for them, and re-layouts: 17.3 us -> 4.94 us
  transfers between devices with their start and end apart: 7 -> 0, of which waited for: 5 -> 0; matrix products, arithmetic and copies ran while one was open for 5% -> 0% of each run, Pallas kernels for 26% -> 0%
where the time goes in v2:
time: 208 us
  Pallas kernels  199 us (96%)
  local copies, waits for them, and re-layouts  8.5 us (4%)
    pallas_call x1, Pallas kernels, body(): pl.pallas_call(mixer_kernel, out_shape=jax.ShapeDtypeStruct((rows, width)...  199 us
    unnamed x3, local copies, waits for them, and re-layouts  4.94 us

profile of v2, /device:TPU:26, one launch (start us, length us, event | category | flops | bytes accessed | tf_op | source)
XLA Modules:
  0.0 208.0 jit_solution(926781658232467166)
XLA Ops:
  0.0 1.5 copy.10
  1.5 0.9 copy.11
  2.4 1.2 copy.13.shard
  3.6 1.4 broadcast_in_dim.2.ids
  5.1 1.5 copy.16
  6.6 199.4 %mixer.1 = bf16[272,1024]{1,0:T(8,128)(2,1)} custom-call(s32[2,136,128]{2,1,0:T(8,128)} %broadcast_in_dim.2.ids, bf16[32,96,128]{2,1,0:T(8,128)(2,1)} %bitcast.14, bf16[128,3072]{1,0:T(8,128)(2,1)} %copy.13.shard, bf16[512,1024]{1,0:T(8,128)(2,1)} %table.1, f32[1,4096]{1,0:T(1,128)} %gain.1, f32[3,7,1024]{2,1,0:T(8,128)} %bitcast.17, f32[128,1024]{1,0:T(8,128)} %bitcast.16, ...), custom_call_target="tpu_custom_call" | custom-call | tf_op jit(solution)/shard_map/mixer/pallas_call | solution.py:735
  206.1 1.9 copy.18

commit v3 on v2

--- a/solution.py
+++ b/solution.py
@@ -30,20 +30,24 @@
         ("c1", "y", True, 0, None),
         ("a2", "up", True, -1, None),
         ("b2", "down", True, 1, None),
+        ("c2", "y", True, -1, 1),
+        ("c3", "y", True, 1, 0),
         ("a3", "up", True, -2, None),
         ("b3", "down", True, 2, None),
-        ("c2", "y", True, -2, 1),
-        ("c3", "y", True, 2, 0),
+        ("c4", "y", True, -2, 1),
+        ("c5", "y", True, 2, 0),
         ("a4", "up", True, -3, 0),
         ("b4", "down", True, 3, 1),
-        ("a5", "up", False, 0, None),
-        ("b5", "down", False, 0, None),
-        ("c4", "y", True, -3, None),
-        ("c5", "y", True, 3, None),
+        ("c6", "y", True, -3, 0),
+        ("c7", "y", True, 3, 1),
+        ("a5", "up", False, 0, 0),
+        ("b5", "down", False, 0, 1),
+        ("c8", "y", True, -3, 1),
+        ("c9", "y", True, 3, 0),
         ("a6", "up", False, -1, 0),
         ("b6", "down", False, 1, 1),
-        ("c6", "y", True, 4, 0),
-        ("c7", "y", True, 4, 1),
+        ("a7", "up", False, -3, 0),
+        ("b7", "down", False, 3, 1),
     )
     COUNT = len(MOVES)
 
@@ -114,34 +118,42 @@
             device_id_type=MESH,
         )
 
-    def run(self, local_sem):
+    def run(self, local_sem, late=None):
         keep = pltpu.make_async_copy(self.own, self.slot(self.block(True, 0), None), local_sem)
         self.start("a1", "b1", "c1")
         self.side_own().start()
         keep.start()
         self.landed("a1")
-        self.start("a2")
+        self.start("a2", "c2")
         self.landed("b1")
-        self.start("b2")
+        self.start("b2", "c3")
         self.landed("c1")
         self.landed("a2")
-        self.start("a3", "c2")
+        self.start("a3", "c4")
         self.landed("b2")
-        self.start("b3", "c3")
-        self.start("a5", "b5")
+        self.start("b3", "c5")
+        self.landed("c2")
+        self.landed("c3")
         self.landed("a3")
-        self.start("a4", "c4")
+        self.start("a4", "c6", "a5")
         self.landed("b3")
-        self.start("b4", "c5")
+        self.start("b4", "c7", "b5")
+        for name in ("c4", "c5", "a4", "b4"):
+            self.landed(name)
+        self.start("c8", "c9")
         self.landed("a5")
         self.start("a6")
         self.landed("b5")
         self.start("b6")
-        self.landed("a4")
-        self.start("c6")
-        self.landed("b4")
-        self.start("c7")
-        for name in ("c2", "c3", "a6", "b6", "c4", "c5", "c6", "c7"):
+        self.landed("c6")
+        self.start("a7")
+        self.landed("c7")
+        self.start("b7")
+        self.landed("a6")
+        self.landed("b6")
+        if late is not None:
+            late()
+        for name in ("c8", "c9", "a7", "b7"):
             self.landed(name)
         keep.wait()
         for at, (name, direction, same, dz, half) in enumerate(self.MOVES):
@@ -171,9 +183,11 @@
     tensor = lax.axis_index("tensor")
     seq = lax.axis_index("seq")
     y, z, core = place()
-    count, share, depth = tail.shape
+    depth = tail.shape[2]
     vocab, width = table.shape
-    wide = share // 3
+    wide = part.shape[1]
+    count = tail.shape[1] // wide
+    share = 3 * wide
     half = vocab // 2
     ways = w.shape[0]
     micro = gf.shape[0]
@@ -183,7 +197,8 @@
     short_taps = se.shape[1]
     lane = 128
     block = 256
-    chunks = ((0, 128), (128, micro * length - 128))
+    chunks = ((0, 64), (64, 64), (128, 80), (208, micro * length - 208))
+    groups = ((0, 128), (128, micro * length - 128))
     ahead = (tensor + 1 + core * (ways - 2)) % ways
     behind = (tensor + ways - 1 - core * (ways - 2)) % ways
     far = (tensor + 2) % ways
@@ -207,7 +222,7 @@
     def short(tile, stream, start, rows):
         total = jnp.zeros((rows, lane), jnp.float32)
         for tap in range(short_taps):
-            total += se[stream, tap : tap + 1, lanes(tile)] * sf[
+            total += se[stream, tap, :, lanes(tile)] * sf[
                 stream, tile, start - tap : start - tap + rows, :
             ]
         return total
@@ -216,18 +231,19 @@
         values = short(tile, 1, start, rows) * short(tile, 2, start, rows)
         gf[mb, tile, at : at + rows, :] = values.astype(jnp.bfloat16).astype(jnp.float32)
 
-    def medium(mb):
+    def medium(mb, begin, rows):
         def one_tile(tile, carry):
-            total = jnp.zeros((length, lane), jnp.float32)
-            reach = length + taps - 8
+            total = jnp.zeros((rows, lane), jnp.float32)
+            reach = rows + taps - 8
             for shift in range(8):
-                begin = length - (taps - 8) - shift
-                window = gf[mb, tile, begin : begin + reach, :]
+                first = length + begin - (taps - 8) - shift
+                window = gf[mb, tile, first : first + reach, :]
                 for step in range(taps // 8):
                     tap = 8 * step + shift
                     at = taps - 8 - 8 * step
-                    total += mr[tap : tap + 1, lanes(tile)] * window[at : at + length]
-            mixf[mb * length : (mb + 1) * length, lanes(tile)] = query[mb, tile] * total
+                    total += mr[tap : tap + 1, lanes(tile)] * window[at : at + rows]
+            to = mb * length + begin
+            mixf[to : to + rows, lanes(tile)] = query[mb, tile, begin : begin + rows] * total
             return carry
 
         lax.fori_loop(0, tiles, one_tile, 0)
@@ -299,7 +315,7 @@
         lax.fori_loop(0, rows // lines, add, 0)
 
     def reduce_close():
-        for chunk in range(2):
+        for chunk in range(len(chunks)):
             hop(chunk, 0, ahead).wait_send()
             hop(chunk, 1, ahead).wait_send()
             hop(chunk, 2, behind).wait_send()
@@ -342,11 +358,14 @@
 
         rows = pl.ds(pl.multiple_of(core * half, half), half)
 
+        def table_of(owner):
+            return w.at[1 + owner // 2, owner % 2, 0:vocab]
+
         def along(at, src, owner, to):
-            return remote(src, w.at[owner, rows, 0:width], x_send.at[at], x_recv.at[at], tensor=to)
+            return remote(src, table_of(owner).at[rows], x_send.at[at], x_recv.at[at], tensor=to)
 
         def across(at, owner):
-            piece = w.at[owner, rows, 0:width]
+            piece = table_of(owner).at[rows]
             return remote(
                 piece, piece, x_send.at[at], x_recv.at[at], seq=seq_of(y, z, 1 - core)
             )
@@ -354,14 +373,14 @@
         mine = table.at[rows]
         along(0, mine, tensor, ahead).start()
         along(1, mine, tensor, behind).start()
-        keep = pltpu.make_async_copy(table, w.at[tensor, 0:vocab, 0:width], local.at[0])
+        keep = pltpu.make_async_copy(table, table_of(tensor), local.at[0])
         keep.start()
 
         def spread(step):
             to = (seq + step) % count
             return remote(
-                tail.at[to],
-                tail_all.at[:, pl.ds(pl.multiple_of(seq * depth, depth), depth)],
+                tail.at[:, pl.ds(pl.multiple_of(to * wide, wide), wide)],
+                tail_all.at[:, :, pl.ds(pl.multiple_of(seq * depth, depth), depth)],
                 a2a_send.at[step], a2a_recv.at[step], seq=to,
             )
 
@@ -371,19 +390,19 @@
 
         lax.fori_loop(1, count, spread_start, 0)
         keep_tail = pltpu.make_async_copy(
-            tail.at[seq],
-            tail_all.at[:, pl.ds(pl.multiple_of(seq * depth, depth), depth)],
+            tail.at[:, pl.ds(pl.multiple_of(seq * wide, wide), wide)],
+            tail_all.at[:, :, pl.ds(pl.multiple_of(seq * depth, depth), depth)],
             local.at[1],
         )
         keep_tail.start()
         ids_all[:, length : 2 * length] = ids[...]
 
         along(0, mine, tensor, ahead).wait_recv()
-        along(2, w.at[behind, rows, 0:width], behind, ahead).start()
+        along(2, table_of(behind).at[rows], behind, ahead).start()
         across(3, behind).start()
         along(1, mine, tensor, behind).wait_recv()
         across(4, ahead).start()
-        got = w.at[far, rows, 0:width]
+        got = table_of(far).at[rows]
         arrival(got, x_recv.at[2])
         across(5, far).start()
         keep.wait()
@@ -401,20 +420,20 @@
             window = pl.ds(pl.multiple_of(at * lines, lines), lines)
             total = jnp.zeros((lines, 1), jnp.float32)
             for way in range(ways):
-                values = w[way, window, 0:width].astype(jnp.float32)
+                values = w[1 + way // 2, way % 2, window].astype(jnp.float32)
                 total += jnp.sum(values * values, axis=1, keepdims=True)
             scale = lax.rsqrt(total / (ways * width) + EPS)
             for way in range(ways):
-                values = w[way, window, 0:width].astype(jnp.float32)
+                values = w[1 + way // 2, way % 2, window].astype(jnp.float32)
                 values = values * scale * gain[:, way * width : (way + 1) * width]
-                w[way, window, 0:width] = values.astype(jnp.bfloat16)
+                w[1 + way // 2, way % 2, window] = values.astype(jnp.bfloat16)
             return carry
 
         lax.fori_loop(0, vocab // lines, normalise, 0)
 
         def spread_wait(step, carry):
             spread(step).wait_send()
-            arrival(tail_all.at[:, pl.ds(0, depth)], a2a_recv.at[step])
+            arrival(tail_all.at[:, :, pl.ds(0, depth)], a2a_recv.at[step])
             return carry
 
         lax.fori_loop(1, count, spread_wait, 0)
@@ -422,8 +441,8 @@
         total = jnp.zeros((share, vocab), jnp.float32)
         for way in range(ways):
             total += lax.dot_general(
-                tail_all[:, way * width : (way + 1) * width],
-                w[way, 0:vocab, 0:width],
+                tail_all[:, :, way * width : (way + 1) * width].reshape(share, width),
+                w[1 + way // 2, way % 2, 0:vocab],
                 (((1,), (1,)), ((), ())),
                 preferred_element_type=jnp.float32,
             )
@@ -435,7 +454,7 @@
             if part_of is not None:
                 some = wide // 2
                 at = at + part_of * some
-            return w.at[0:3, pl.ds(pl.multiple_of(at, some), some), width : width + vocab]
+            return w.at[0, :, pl.ds(pl.multiple_of(at, some), some), 0:vocab]
 
         Gather(slot, part, send, recv, side_send, side_recv).run(local.at[0])
         load_weight.wait()
@@ -444,20 +463,20 @@
         def _():
             ids_on.wait_recv()
 
-        onehot = w.at[3, 0 : 2 * length, width : width + vocab]
+        onehot = w.at[3, 0, 0 : 2 * length, 0:vocab]
 
         def streams(mb):
             for part_at in range(vocab // lane):
                 number = lax.broadcasted_iota(jnp.int32, (2 * length, lane), 1) + part_at * lane
                 hit = jnp.where(ids_all[mb] == number, 1.0, 0.0).astype(jnp.bfloat16)
-                w[3, 0 : 2 * length, width + part_at * lane : width + (part_at + 1) * lane] = hit
+                w[3, 0, 0 : 2 * length, part_at * lane : (part_at + 1) * lane] = hit
 
             def one_block(at, carry):
                 stream, inner = at // (width // block), at % (width // block)
                 columns = pl.ds(pl.multiple_of(inner * block, block), block)
                 values = lax.dot_general(
                     onehot[...],
-                    w[stream, columns, width : width + vocab],
+                    w[0, stream, columns, 0:vocab],
                     (((1,), (1,)), ((), ())),
                     preferred_element_type=jnp.float32,
                 ).astype(jnp.bfloat16).astype(jnp.float32)
@@ -488,21 +507,31 @@
             lax.fori_loop(0, tiles, one_tile, 0)
 
         sf[:, :, 0:8, :] = jnp.zeros((3, tiles, 8, lane), jnp.float32)
+        def pass_on(chunk):
+            reduce_end(chunk)
+            relay(chunk).start()
+
         streams(0)
-        medium(0)
+        medium(0, 0, 64)
         reduce_start(0)
+        medium(0, 64, length - 64)
+        reduce_start(1)
+        reduce_middle(0)
         streams(1)
-        reduce_middle(0)
-        medium(1)
-        reduce_end(0)
-        relay(0).start()
-        reduce_start(1)
         reduce_middle(1)
-        reduce_end(1)
-        relay(1).start()
+        pass_on(0)
+        medium(1, 0, 208 - length)
+        reduce_start(2)
+        pass_on(1)
+        medium(1, 208 - length, 2 * length - 208)
+        reduce_start(3)
+        reduce_middle(2)
+        reduce_middle(3)
+        pass_on(2)
+        pass_on(3)
         reduce_close()
-        relay(0).wait_send()
-        relay(1).wait_send()
+        for chunk in range(len(chunks)):
+            relay(chunk).wait_send()
 
         @pl.when(seq < count - 1)
         def _():
@@ -538,10 +567,7 @@
             if part_of is not None:
                 some = depth // 2
                 at = at + part_of * some
-            return w.at[owner // per, pl.ds(pl.multiple_of(at, some), some)]
-
-        Gather(slot, shard, send, recv, side_send, side_recv).run(local.at[0])
-        load_weight.wait()
+            return w.at[owner // per, :, pl.ds(pl.multiple_of(at, some), some)]
 
         def share_out(chunk, at, owner, to):
             first, rows = chunks[chunk]
@@ -567,13 +593,13 @@
             arrival(xs.at[far, first : first + rows], ag_recv.at[chunk * 3 + 2])
 
         def gather_close():
-            for chunk in range(2):
+            for chunk in range(len(chunks)):
                 share_out(chunk, 0, tensor, ahead).wait_send()
                 share_out(chunk, 1, tensor, behind).wait_send()
                 share_out(chunk, 2, behind, ahead).wait_send()
 
-        def project(chunk):
-            first, rows = chunks[chunk]
+        def project(group):
+            first, rows = groups[group]
             lines = 16
 
             def normalise(at, carry):
@@ -594,12 +620,12 @@
 
             def one_block(at, carry):
                 stream, inner = at // (width // block), at % (width // block)
-                columns = pl.ds(pl.multiple_of(at * block, block), block)
+                columns = pl.ds(pl.multiple_of(inner * block, block), block)
                 total = jnp.zeros((rows, block), jnp.float32)
                 for way in range(ways):
                     total += jnp.dot(
                         xn[way, first : first + rows],
-                        w[way, :, columns],
+                        w[way, stream, :, columns],
                         preferred_element_type=jnp.float32,
                     )
                 total = total.astype(jnp.bfloat16).astype(jnp.float32)
@@ -681,28 +707,46 @@
             def _():
                 gf[mb, :, 0:length, :] = jnp.zeros((tiles, length, lane), jnp.float32)
 
-        gather_start(0)
-        gather_middle(0)
+        def early():
+            gather_start(0)
+            gather_middle(0)
+            gather_start(1)
+
+        Gather(slot, shard, send, recv, side_send, side_recv).run(local.at[0], early)
+        load_weight.wait()
+        gather_middle(1)
         gather_end(0)
-        gather_start(1)
+        gather_end(1)
         project(0)
-        gather_middle(1)
-        gather_end(1)
+        gather_start(2)
+        gather_start(3)
+        gather_middle(2)
+        gather_middle(3)
+        gather_end(2)
+        gather_end(3)
         project(1)
         rim_start(0)
         rim_start(1)
         shorts(0)
         shorts(1)
         gated_end(0)
-        medium(0)
+        medium(0, 0, 64)
         reduce_start(0)
+        medium(0, 64, length - 64)
+        reduce_start(1)
+        reduce_middle(0)
         gated_end(1)
-        reduce_middle(0)
-        medium(1)
+        medium(1, 0, 208 - length)
+        reduce_start(2)
+        reduce_middle(1)
         reduce_end(0)
-        reduce_start(1)
-        reduce_middle(1)
+        medium(1, 208 - length, 2 * length - 208)
+        reduce_start(3)
         reduce_end(1)
+        reduce_middle(2)
+        reduce_middle(3)
+        reduce_end(2)
+        reduce_end(3)
         reduce_close()
         gather_close()
 
@@ -724,10 +768,9 @@
     rows = micro * length
     taps = mr_filter.shape[1]
     depth = in_weight.shape[1]
-    share = 3 * width // count
-    shard = in_weight[0].reshape(depth, 3 * width)
-    tail = in_weight[0].reshape(depth, 3, count, width // count).transpose(2, 1, 3, 0)
-    tail = tail.reshape(count, share, depth)
+    wide = width // count
+    shard = in_weight[0].transpose(1, 0, 2)
+    tail = shard.transpose(0, 2, 1)
     ids = jnp.broadcast_to(token_ids[:, :, None], (micro, length, lane))
     moves = Gather.COUNT
     bf16, f32 = jnp.bfloat16, jnp.float32
@@ -738,10 +781,10 @@
         in_specs=[VMEM, HBM, HBM, VMEM, VMEM, VMEM, VMEM, HBM],
         out_specs=VMEM,
         scratch_shapes=[
-            scratch((ways, width, 3 * width), bf16),
+            scratch((ways, 3, width, width), bf16),
             scratch((width, full), bf16),
-            scratch((share, full), bf16),
-            scratch((3, share // 3, vocab), bf16),
+            scratch((3, wide, full), bf16),
+            scratch((3, wide, vocab), bf16),
             scratch((micro, 2 * length, lane), jnp.int32),
             scratch((3, tiles, 2 * length + 16, lane), f32),
             scratch((micro, tiles, 2 * length, lane), f32),
@@ -766,12 +809,12 @@
             dma((count,)),
             dma((6,)),
             dma((6,)),
-            dma((6,)),
-            dma((6,)),
-            dma((6,)),
-            dma((6,)),
-            dma((2,)),
-            dma((2,)),
+            dma((12,)),
+            dma((12,)),
+            dma((12,)),
+            dma((12,)),
+            dma((4,)),
+            dma((4,)),
             dma((2 * micro,)),
             dma((2 * micro,)),
             dma((3,)),
@@ -780,7 +823,7 @@
             collective_id=0, has_side_effects=True, vmem_limit_bytes=60 << 20
         ),
         name="mixer",
-    )(ids, tail, shard, embed_table, norm_gain, se_filter[0], mr_filter[0], out_weight[0])
+    )(ids, tail, shard, embed_table, norm_gain, se_filter[0][:, :, None], mr_filter[0], out_weight[0])
     return result.reshape(1, micro, length, width)
 
 

time: 208 us -> 186 us (0.89)
  Pallas kernels: 199 us -> 180 us
  local copies, waits for them, and re-layouts: 8.5 us -> 5.62 us
    pallas_call x1, Pallas kernels: 199 us -> 180 us  [body(): pl.pallas_call(mixer_kernel, out_shape=jax.ShapeDtypeStruct((rows, width)...]
    unnamed x3 -> x1, local copies, waits for them, and re-layouts: 4.94 us -> 1.89 us
where the time goes in v3:
time: 186 us
  Pallas kernels  180 us (97%)
  local copies, waits for them, and re-layouts  5.62 us (3%)
    pallas_call x1, Pallas kernels, body(): pl.pallas_call(mixer_kernel, out_shape=jax.ShapeDtypeStruct((rows, width)...  180 us

profile of v3, /device:TPU:26, one launch (start us, length us, event | category | flops | bytes accessed | tf_op | source)
XLA Modules:
  0.0 185.5 jit_solution(7645270263252638375)
XLA Ops:
  0.0 1.4 broadcast_in_dim.2.ids
  1.4 2.3 %copy.8.tail = bf16[3,1024,128]{2,1,0:T(8,128)(2,1)} copy(bf16[3,1024,128]{1,2,0:T(8,128)(2,1)} %bitcast.10) | data formatting | bytes 1572864 | tf_op jit(solution)/shard_map/transpose;transpose | solution.py:773
  3.7 179.9 %mixer.1 = bf16[272,1024]{1,0:T(8,128)(2,1)} custom-call(s32[2,136,128]{2,1,0:T(8,128)} %broadcast_in_dim.2.ids, bf16[3,1024,128]{2,1,0:T(8,128)(2,1)} %copy.8.tail, bf16[3,128,1024]{2,1,0:T(8,128)(2,1)} %bitcast.11, bf16[512,1024]{1,0:T(8,128)(2,1)} %table.1, f32[1,4096]{1,0:T(1,128)} %gain.1, f32[3,7,1,1024]{3,2,1,0:T(1,128)} %bitcast.14, ...), custom_call_target="tpu_custom_call" | custom-call | tf_op jit(solution)/shard_map/mixer/pallas_call | solution.py:778
  183.6 1.9 %copy.10 = bf16[1,2,136,1024]{3,2,1,0:T(8,128)(2,1)} copy(bf16[1,2,136,1024]{3,2,1,0:T(8,128)(2,1)} %bitcast.12) | data formatting | bytes 1114112

commit v4 on v3

--- a/solution.py
+++ b/solution.py
@@ -197,8 +197,11 @@
     short_taps = se.shape[1]
     lane = 128
     block = 256
-    chunks = ((0, 64), (64, 64), (128, 80), (208, micro * length - 208))
-    groups = ((0, 128), (128, micro * length - 128))
+    broad = 512
+    pitch = length + 8
+    chunks = ((0, 64), (64, pitch - 64), (pitch, 80), (pitch + 80, pitch - 80))
+    fine = tuple((at, *chunk) for at, chunk in enumerate(chunks))
+    coarse = ((0, 0, pitch),) + tuple((at - 1, *chunks[at]) for at in (2, 3))
     ahead = (tensor + 1 + core * (ways - 2)) % ways
     behind = (tensor + ways - 1 - core * (ways - 2)) % ways
     far = (tensor + 2) % ways
@@ -234,39 +237,40 @@
     def medium(mb, begin, rows):
         def one_tile(tile, carry):
             total = jnp.zeros((rows, lane), jnp.float32)
-            reach = rows + taps - 8
+            first = length + begin - taps
+            window = gf[mb, tile, first : first + rows + taps, :]
             for shift in range(8):
-                first = length + begin - (taps - 8) - shift
-                window = gf[mb, tile, first : first + reach, :]
+                part_sum = jnp.zeros((rows + 8, lane), jnp.float32)
                 for step in range(taps // 8):
                     tap = 8 * step + shift
                     at = taps - 8 - 8 * step
-                    total += mr[tap : tap + 1, lanes(tile)] * window[at : at + rows]
-            to = mb * length + begin
+                    part_sum += mr[tap : tap + 1, lanes(tile)] * window[at : at + rows + 8]
+                total += part_sum[8 - shift : 8 - shift + rows]
+            to = mb * pitch + begin
             mixf[to : to + rows, lanes(tile)] = query[mb, tile, begin : begin + rows] * total
             return carry
 
         lax.fori_loop(0, tiles, one_tile, 0)
 
     def partial_to(chunk, owner, finish):
-        first, rows = chunks[chunk]
+        index, first, rows = chunk
         window = slice(first, first + rows)
 
         def one_block(at, carry):
-            inner = pl.ds(pl.multiple_of(at * block, block), block)
-            outer = pl.ds(pl.multiple_of(owner * width + at * block, block), block)
+            inner = pl.ds(pl.multiple_of(at * broad, broad), broad)
+            outer = pl.ds(pl.multiple_of(owner * width + at * broad, broad), broad)
             term = jnp.dot(mixed[window], weight[:, outer], preferred_element_type=jnp.float32)
             finish(window, inner, term)
             return carry
 
-        lax.fori_loop(0, width // block, one_block, 0)
+        lax.fori_loop(0, width // broad, one_block, 0)
 
     def hop(chunk, at, to):
-        first, rows = chunks[chunk]
+        index, first, rows = chunk
         window = slice(first, first + rows)
         return remote(
             send_buf.at[at, window], recv_buf.at[at, window],
-            rs_send.at[chunk * 3 + at], rs_recv.at[chunk * 3 + at], tensor=to,
+            rs_send.at[index * 3 + at], rs_recv.at[index * 3 + at], tensor=to,
         )
 
     def fill(at):
@@ -276,7 +280,7 @@
         return finish
 
     def reduce_start(chunk):
-        first, rows = chunks[chunk]
+        index, first, rows = chunk
         window = slice(first, first + rows)
         mixed[window] = mixf[window].astype(jnp.bfloat16)
         partial_to(chunk, far, fill(0))
@@ -300,7 +304,7 @@
         partial_to(chunk, tensor, keep)
 
     def reduce_end(chunk):
-        first, rows = chunks[chunk]
+        index, first, rows = chunk
         hop(chunk, 2, behind).wait_recv()
         hop(chunk, 1, ahead).wait_recv()
         lines = 16
@@ -314,8 +318,8 @@
 
         lax.fori_loop(0, rows // lines, add, 0)
 
-    def reduce_close():
-        for chunk in range(len(chunks)):
+    def reduce_close(pieces):
+        for chunk in pieces:
             hop(chunk, 0, ahead).wait_send()
             hop(chunk, 1, ahead).wait_send()
             hop(chunk, 2, behind).wait_send()
@@ -493,7 +497,7 @@
                 values = jnp.dot(
                     onehot[...], table[:, columns], preferred_element_type=jnp.float32
                 )
-                base[mb * length : (mb + 1) * length, columns] = values[length : 2 * length]
+                base[mb * pitch : mb * pitch + length, columns] = values[length : 2 * length]
                 return carry
 
             lax.fori_loop(0, width // block, own_rows, 0)
@@ -508,28 +512,28 @@
 
         sf[:, :, 0:8, :] = jnp.zeros((3, tiles, 8, lane), jnp.float32)
         def pass_on(chunk):
-            reduce_end(chunk)
+            reduce_end(fine[chunk])
             relay(chunk).start()
 
         streams(0)
         medium(0, 0, 64)
-        reduce_start(0)
+        reduce_start(fine[0])
         medium(0, 64, length - 64)
-        reduce_start(1)
-        reduce_middle(0)
+        reduce_start(fine[1])
+        reduce_middle(fine[0])
         streams(1)
-        reduce_middle(1)
+        reduce_middle(fine[1])
         pass_on(0)
-        medium(1, 0, 208 - length)
-        reduce_start(2)
+        medium(1, 0, 80)
+        reduce_start(fine[2])
         pass_on(1)
-        medium(1, 208 - length, 2 * length - 208)
-        reduce_start(3)
-        reduce_middle(2)
-        reduce_middle(3)
+        medium(1, 80, length - 80)
+        reduce_start(fine[3])
+        reduce_middle(fine[2])
+        reduce_middle(fine[3])
         pass_on(2)
         pass_on(3)
-        reduce_close()
+        reduce_close(fine)
         for chunk in range(len(chunks)):
             relay(chunk).wait_send()
 
@@ -599,7 +603,7 @@
                 share_out(chunk, 2, behind, ahead).wait_send()
 
         def project(group):
-            first, rows = groups[group]
+            first, rows = group * pitch, pitch
             lines = 16
 
             def normalise(at, carry):
@@ -632,14 +636,7 @@
                 for side in range(block // lane):
                     tile = inner * (block // lane) + side
                     piece = total[:, side * lane : (side + 1) * lane]
-                    for mb in range(micro):
-                        begin = max(first, mb * length)
-                        end = min(first + rows, (mb + 1) * length)
-                        if begin < end:
-                            to = mb * (length + 8) + 8 + begin - mb * length
-                            sf[stream, tile, to : to + end - begin, :] = piece[
-                                begin - first : end - first
-                            ]
+                    sf[stream, tile, first + 8 : first + 8 + length, :] = piece[0:length]
                 return carry
 
             lax.fori_loop(0, 3 * width // block, one_block, 0)
@@ -657,7 +654,7 @@
             )
 
         def rim_start(mb):
-            last = (mb + 1) * (length + 8)
+            last = (mb + 1) * pitch
             rim_send[mb] = sf[:, :, last - 16 : last, :].astype(jnp.bfloat16)
 
             @pl.when(seq < count - 1)
@@ -665,7 +662,7 @@
                 rim(mb).start()
 
         def shorts(mb):
-            first = mb * (length + 8)
+            first = mb * pitch
 
             @pl.when(seq > 0)
             def _():
@@ -718,36 +715,33 @@
         gather_end(0)
         gather_end(1)
         project(0)
+        rim_start(0)
         gather_start(2)
+        shorts(0)
+        gather_middle(2)
         gather_start(3)
-        gather_middle(2)
+        gated_end(0)
+        medium(0, 0, 64)
         gather_middle(3)
+        medium(0, 64, length - 64)
+        reduce_start(coarse[0])
         gather_end(2)
         gather_end(3)
         project(1)
-        rim_start(0)
         rim_start(1)
-        shorts(0)
+        reduce_middle(coarse[0])
         shorts(1)
-        gated_end(0)
-        medium(0, 0, 64)
-        reduce_start(0)
-        medium(0, 64, length - 64)
-        reduce_start(1)
-        reduce_middle(0)
         gated_end(1)
-        medium(1, 0, 208 - length)
-        reduce_start(2)
-        reduce_middle(1)
-        reduce_end(0)
-        medium(1, 208 - length, 2 * length - 208)
-        reduce_start(3)
-        reduce_end(1)
-        reduce_middle(2)
-        reduce_middle(3)
-        reduce_end(2)
-        reduce_end(3)
-        reduce_close()
+        medium(1, 0, 80)
+        reduce_start(coarse[1])
+        medium(1, 80, length - 80)
+        reduce_start(coarse[2])
+        reduce_middle(coarse[1])
+        reduce_middle(coarse[2])
+        reduce_end(coarse[0])
+        reduce_end(coarse[1])
+        reduce_end(coarse[2])
+        reduce_close(coarse)
         gather_close()
 
         @pl.when(seq < count - 1)
@@ -765,7 +759,7 @@
     ways = full // width
     lane = 128
     tiles = width // lane
-    rows = micro * length
+    rows = micro * (length + 8)
     taps = mr_filter.shape[1]
     depth = in_weight.shape[1]
     wide = width // count
@@ -824,7 +818,7 @@
         ),
         name="mixer",
     )(ids, tail, shard, embed_table, norm_gain, se_filter[0][:, :, None], mr_filter[0], out_weight[0])
-    return result.reshape(1, micro, length, width)
+    return result.reshape(1, micro, length + 8, width)[:, :, :length]
 
 
 def solution(mesh):

time: 186 us -> 171 us (0.919)
  Pallas kernels: 180 us -> 165 us
    pallas_call x1, Pallas kernels: 180 us -> 165 us  [body(): pl.pallas_call(mixer_kernel, out_shape=jax.ShapeDtypeStruct((rows, width)...]
    slice x0 -> x1, local copies, waits for them, and re-layouts: none -> 1.9 us  [body(): return result.reshape(1, micro, length + 8, width)[:, :, :length]]
    unnamed x1 -> x0, local copies, waits for them, and re-layouts: 1.89 us -> none
where the time goes in v4:
time: 171 us
  Pallas kernels  165 us (96%)
  local copies, waits for them, and re-layouts  5.62 us (3%)
    pallas_call x1, Pallas kernels, body(): pl.pallas_call(mixer_kernel, out_shape=jax.ShapeDtypeStruct((rows, width)...  165 us

profile of v4, /device:TPU:26, one launch (start us, length us, event | category | flops | bytes accessed | tf_op | source)
XLA Modules:
  0.0 170.6 jit_solution(2561655205940793246)
XLA Ops:
  0.0 1.4 broadcast_in_dim.2.ids
  1.4 2.3 %copy.8.tail = bf16[3,1024,128]{2,1,0:T(8,128)(2,1)} copy(bf16[3,1024,128]{1,2,0:T(8,128)(2,1)} %bitcast.10) | data formatting | bytes 1572864 | tf_op jit(solution)/shard_map/transpose;transpose | solution.py:767
  3.7 165.0 %mixer.1 = bf16[288,1024]{1,0:T(8,128)(2,1)} custom-call(s32[2,136,128]{2,1,0:T(8,128)} %broadcast_in_dim.2.ids, bf16[3,1024,128]{2,1,0:T(8,128)(2,1)} %copy.8.tail, bf16[3,128,1024]{2,1,0:T(8,128)(2,1)} %bitcast.11, bf16[512,1024]{1,0:T(8,128)(2,1)} %table.1, f32[1,4096]{1,0:T(1,128)} %gain.1, f32[3,7,1,1024]{3,2,1,0:T(1,128)} %bitcast.14, ...), custom_call_target="tpu_custom_call" | custom-call | tf_op jit(solution)/shard_map/mixer/pallas_call | solution.py:772
  168.7 1.9 %slice.4 = bf16[1,2,136,1024]{3,2,1,0:T(8,128)(2,1)} slice(bf16[1,2,144,1024]{3,2,1,0:T(8,128)(2,1)} %bitcast.12), slice={[0:1], [0:2], [0:136], [0:1024]} | slice | bytes 1114112 | tf_op jit(solution)/shard_map/slice | solution.py:821

commit v5 on v4

--- a/solution.py
+++ b/solution.py
@@ -173,7 +173,7 @@
 
 
 def mixer_kernel(
-    ids, tail, shard, table, gain, se, mr, weight_hbm, out,
+    ids, shard, table, gain, se, mr, weight_hbm, out,
     w, weight, tail_all, part, ids_all, sf, gf, query, mixf, mixed, send_buf, recv_buf, own_part, base, xs, xn,
     rim_send, rim_recv, far_send, far_recv,
     send, recv, side_send, side_recv, a2a_send, a2a_recv, x_send, x_recv,
@@ -183,10 +183,10 @@
     tensor = lax.axis_index("tensor")
     seq = lax.axis_index("seq")
     y, z, core = place()
-    depth = tail.shape[2]
+    depth = shard.shape[1]
     vocab, width = table.shape
     wide = part.shape[1]
-    count = tail.shape[1] // wide
+    count = width // wide
     share = 3 * wide
     half = vocab // 2
     ways = w.shape[0]
@@ -343,12 +343,24 @@
             greet(seq=(seq + step) % count)
             return carry
 
+        load_shard = pltpu.make_async_copy(shard, xn.at[0:3, 0:depth], local.at[0])
+        load_shard.start()
         lax.fori_loop(1, count, greet_seq, 0)
+        load_shard.wait()
+        tail = w.at[3, :, :, vocab : vocab + depth]
+        for stream in range(3):
+            w[3, stream, :, vocab : vocab + depth] = xn[stream, 0:depth].T
+        for mb in range(micro):
+            for begin, rows in ((0, lane), (lane, length - lane)):
+                line = ids[mb : mb + 1, begin : begin + rows]
+                ids_all[mb, length + begin : length + begin + rows] = jnp.broadcast_to(
+                    line, (lane, rows)
+                ).T
         pl.semaphore_wait(barrier, count + 2)
         load_weight.start()
 
         ids_on = remote(
-            ids, ids_all.at[:, 0:length], halo_send.at[0], halo_recv.at[0],
+            ids_all.at[:, length : 2 * length], ids_all.at[:, 0:length], halo_send.at[0], halo_recv.at[0],
             seq=(seq + 1) % count,
         )
 
@@ -399,7 +411,6 @@
             local.at[1],
         )
         keep_tail.start()
-        ids_all[:, length : 2 * length] = ids[...]
 
         along(0, mine, tensor, ahead).wait_recv()
         along(2, table_of(behind).at[rows], behind, ahead).start()
@@ -664,6 +675,19 @@
         def shorts(mb):
             first = mb * pitch
 
+            def one_gate(tile, carry):
+                gate(mb, tile, first + 16, length - 8, length + 8)
+                far_send[mb, tile] = gf[mb, tile, 2 * length - taps : 2 * length, :].astype(
+                    jnp.bfloat16
+                )
+                return carry
+
+            lax.fori_loop(0, tiles, one_gate, 0)
+
+            @pl.when(seq < count - 1)
+            def _():
+                gated_rim(mb).start()
+
             @pl.when(seq > 0)
             def _():
                 rim(mb).wait_recv()
@@ -674,18 +698,11 @@
                 sf[:, :, first : first + 8, :] = jnp.zeros((3, tiles, 8, lane), jnp.float32)
 
             def one_tile(tile, carry):
+                gate(mb, tile, first + 8, 8, length)
                 query[mb, tile] = short(tile, 0, first + 8, length)
-                gate(mb, tile, first + 8, length, length)
-                far_send[mb, tile] = gf[mb, tile, 2 * length - taps : 2 * length, :].astype(
-                    jnp.bfloat16
-                )
                 return carry
 
             lax.fori_loop(0, tiles, one_tile, 0)
-
-            @pl.when(seq < count - 1)
-            def _():
-                gated_rim(mb).start()
 
         def gated_end(mb):
             @pl.when(seq > 0)
@@ -764,15 +781,13 @@
     depth = in_weight.shape[1]
     wide = width // count
     shard = in_weight[0].transpose(1, 0, 2)
-    tail = shard.transpose(0, 2, 1)
-    ids = jnp.broadcast_to(token_ids[:, :, None], (micro, length, lane))
     moves = Gather.COUNT
     bf16, f32 = jnp.bfloat16, jnp.float32
     scratch, dma = pltpu.VMEM, pltpu.SemaphoreType.DMA
     result = pl.pallas_call(
         mixer_kernel,
         out_shape=jax.ShapeDtypeStruct((rows, width), bf16),
-        in_specs=[VMEM, HBM, HBM, VMEM, VMEM, VMEM, VMEM, HBM],
+        in_specs=[VMEM, HBM, VMEM, VMEM, VMEM, VMEM, HBM],
         out_specs=VMEM,
         scratch_shapes=[
             scratch((ways, 3, width, width), bf16),
@@ -817,7 +832,7 @@
             collective_id=0, has_side_effects=True, vmem_limit_bytes=60 << 20
         ),
         name="mixer",
-    )(ids, tail, shard, embed_table, norm_gain, se_filter[0][:, :, None], mr_filter[0], out_weight[0])
+    )(token_ids, shard, embed_table, norm_gain, se_filter[0][:, :, None], mr_filter[0], out_weight[0])
     return result.reshape(1, micro, length + 8, width)[:, :, :length]
 
 

time: 171 us -> 165 us (0.965)
  local copies, waits for them, and re-layouts: 5.62 us -> 1.9 us
  Pallas kernels: 165 us -> 163 us
    another operation x1 -> x0, local copies, waits for them, and re-layouts: 2.28 us -> none  [body(): tail = shard.transpose(0, 2, 1)]
    pallas_call x1, Pallas kernels: 165 us -> 163 us  [body(): pl.pallas_call(mixer_kernel, out_shape=jax.ShapeDtypeStruct((rows, width)...]
where the time goes in v5:
time: 165 us
  Pallas kernels  163 us (99%)
  local copies, waits for them, and re-layouts  1.9 us (1%)
    pallas_call x1, Pallas kernels, body(): pl.pallas_call(mixer_kernel, out_shape=jax.ShapeDtypeStruct((rows, width)...  163 us

profile of v5, /device:TPU:26, one launch (start us, length us, event | category | flops | bytes accessed | tf_op | source)
XLA Modules:
  0.0 164.7 jit_solution(5090212936386684795)
XLA Ops:
  0.0 162.8 %mixer.1 = bf16[288,1024]{1,0:T(8,128)(2,1)} custom-call(s32[2,136]{1,0:T(2,128)} %ids.1, bf16[3,128,1024]{2,1,0:T(8,128)(2,1)} %bitcast.9, bf16[512,1024]{1,0:T(8,128)(2,1)} %table.1, f32[1,4096]{1,0:T(1,128)} %gain.1, f32[3,7,1,1024]{3,2,1,0:T(1,128)} %bitcast.11, f32[128,1024]{1,0:T(8,128)} %bitcast.10, bf16[1024,4096]{1,0:T(8,128)(2,1)} %bitcast.7), custom_call_target="tpu_custom_call" | custom-call | tf_op jit(solution)/shard_map/mixer/pallas_call | solution.py:787
  162.8 1.9 %slice.4 = bf16[1,2,136,1024]{3,2,1,0:T(8,128)(2,1)} slice(bf16[1,2,144,1024]{3,2,1,0:T(8,128)(2,1)} %bitcast.8), slice={[0:1], [0:2], [0:136], [0:1024]} | slice | bytes 1114112 | tf_op jit(solution)/shard_map/slice | solution.py:836

commit v6 on v5

--- a/solution.py
+++ b/solution.py
@@ -157,19 +157,23 @@
             self.landed(name)
         keep.wait()
         for at, (name, direction, same, dz, half) in enumerate(self.MOVES):
-            self.copy(name).wait_send()
-            if direction == "y":
-                block = (not same, dz)
-            else:
-                block = (same, dz + (-1 if direction == "up" else 1))
-            mine = self.slot(self.block(*block), half)
-            pltpu.make_async_copy(mine, mine, self.side_send.at[at]).wait()
-            other = self.slot(self.block(*block, 1 - self.core), half)
+            other = self.slot(self.block(*self.came(at), 1 - self.core), half)
             pltpu.make_async_copy(other, other, self.side_recv.at[at]).wait()
-        side = self.side_own()
-        side.wait_send()
         other = self.slot(self.block(True, 0, 1 - self.core), None)
         pltpu.make_async_copy(other, other, self.side_recv.at[self.COUNT]).wait()
+
+    def came(self, at):
+        _, direction, same, dz, _ = self.MOVES[at]
+        if direction == "y":
+            return not same, dz
+        return same, dz + (-1 if direction == "up" else 1)
+
+    def close(self):
+        for at, (name, direction, same, dz, half) in enumerate(self.MOVES):
+            self.copy(name).wait_send()
+            mine = self.slot(self.block(*self.came(at)), half)
+            pltpu.make_async_copy(mine, mine, self.side_send.at[at]).wait()
+        self.side_own().wait_send()
 
 
 def mixer_kernel(
@@ -196,7 +200,7 @@
     taps = mr.shape[0]
     short_taps = se.shape[1]
     lane = 128
-    block = 256
+    block = 512
     broad = 512
     pitch = length + 8
     chunks = ((0, 64), (64, pitch - 64), (pitch, 80), (pitch + 80, pitch - 80))
@@ -288,20 +292,28 @@
         partial_to(chunk, behind, fill(2))
         hop(chunk, 2, behind).start()
 
-    def reduce_middle(chunk):
-        hop(chunk, 0, ahead).wait_recv()
-
-        def finish(window, inner, term):
-            both = term + recv_buf[0, window, inner].astype(jnp.float32)
-            send_buf[1, window, inner] = both.astype(jnp.bfloat16)
-
-        partial_to(chunk, ahead, finish)
-        hop(chunk, 1, ahead).start()
+        def onward(window, inner, term):
+            mixf[window, inner] = term
 
         def keep(window, inner, term):
             own_part[window, inner] = term
 
+        partial_to(chunk, ahead, onward)
         partial_to(chunk, tensor, keep)
+
+    def reduce_middle(chunk):
+        index, first, rows = chunk
+        hop(chunk, 0, ahead).wait_recv()
+        lines = 16
+
+        def join(at, carry):
+            window = pl.ds(pl.multiple_of(first + at * lines, lines), lines)
+            both = mixf[window] + recv_buf[0, window].astype(jnp.float32)
+            send_buf[1, window] = both.astype(jnp.bfloat16)
+            return carry
+
+        lax.fori_loop(0, rows // lines, join, 0)
+        hop(chunk, 1, ahead).start()
 
     def reduce_end(chunk):
         index, first, rows = chunk
@@ -471,7 +483,8 @@
                 at = at + part_of * some
             return w.at[0, :, pl.ds(pl.multiple_of(at, some), some), 0:vocab]
 
-        Gather(slot, part, send, recv, side_send, side_recv).run(local.at[0])
+        spread_table = Gather(slot, part, send, recv, side_send, side_recv)
+        spread_table.run(local.at[0])
         load_weight.wait()
 
         @pl.when(seq > 0)
@@ -539,12 +552,13 @@
         reduce_start(fine[2])
         pass_on(1)
         medium(1, 80, length - 80)
+        reduce_middle(fine[2])
         reduce_start(fine[3])
-        reduce_middle(fine[2])
         reduce_middle(fine[3])
         pass_on(2)
         pass_on(3)
         reduce_close(fine)
+        spread_table.close()
         for chunk in range(len(chunks)):
             relay(chunk).wait_send()
 
@@ -726,7 +740,8 @@
             gather_middle(0)
             gather_start(1)
 
-        Gather(slot, shard, send, recv, side_send, side_recv).run(local.at[0], early)
+        spread_weight = Gather(slot, shard, send, recv, side_send, side_recv)
+        spread_weight.run(local.at[0], early)
         load_weight.wait()
         gather_middle(1)
         gather_end(0)
@@ -737,6 +752,7 @@
         shorts(0)
         gather_middle(2)
         gather_start(3)
+        spread_weight.close()
         gated_end(0)
         medium(0, 0, 64)
         gather_middle(3)
@@ -752,14 +768,14 @@
         medium(1, 0, 80)
         reduce_start(coarse[1])
         medium(1, 80, length - 80)
+        reduce_middle(coarse[1])
         reduce_start(coarse[2])
-        reduce_middle(coarse[1])
         reduce_middle(coarse[2])
+        gather_close()
         reduce_end(coarse[0])
         reduce_end(coarse[1])
         reduce_end(coarse[2])
         reduce_close(coarse)
-        gather_close()
 
         @pl.when(seq < count - 1)
         def _():

time: 165 us -> 164 us (level)
  no operation moved by 1% of the time
where the time goes in v6:
time: 164 us
  Pallas kernels  162 us (99%)
  local copies, waits for them, and re-layouts  1.9 us (1%)
    pallas_call x1, Pallas kernels, body(): pl.pallas_call(mixer_kernel, out_shape=jax.ShapeDtypeStruct((rows, width)...  162 us

profile of v6, /device:TPU:26, one launch (start us, length us, event | category | flops | bytes accessed | tf_op | source)
XLA Modules:
  0.0 163.7 jit_solution(7988099457239541656)
XLA Ops:
  0.0 161.8 %mixer.1 = bf16[288,1024]{1,0:T(8,128)(2,1)} custom-call(s32[2,136]{1,0:T(2,128)} %ids.1, bf16[3,128,1024]{2,1,0:T(8,128)(2,1)} %bitcast.9, bf16[512,1024]{1,0:T(8,128)(2,1)} %table.1, f32[1,4096]{1,0:T(1,128)} %gain.1, f32[3,7,1,1024]{3,2,1,0:T(1,128)} %bitcast.11, f32[128,1024]{1,0:T(8,128)} %bitcast.10, bf16[1024,4096]{1,0:T(8,128)(2,1)} %bitcast.7), custom_call_target="tpu_custom_call" | custom-call | tf_op jit(solution)/shard_map/mixer/pallas_call | solution.py:803
  161.8 1.9 %slice.4 = bf16[1,2,136,1024]{3,2,1,0:T(8,128)(2,1)} slice(bf16[1,2,144,1024]{3,2,1,0:T(8,128)(2,1)} %bitcast.8), slice={[0:1], [0:2], [0:136], [0:1024]} | slice | bytes 1114112 | tf_op jit(solution)/shard_map/slice | solution.py:852

commit v7 on v6

--- a/solution.py
+++ b/solution.py
@@ -118,7 +118,7 @@
             device_id_type=MESH,
         )
 
-    def run(self, local_sem, late=None):
+    def run(self, local_sem, late=None, last=None):
         keep = pltpu.make_async_copy(self.own, self.slot(self.block(True, 0), None), local_sem)
         self.start("a1", "b1", "c1")
         self.side_own().start()
@@ -153,8 +153,12 @@
         self.landed("b6")
         if late is not None:
             late()
-        for name in ("c8", "c9", "a7", "b7"):
-            self.landed(name)
+        self.landed("c8")
+        self.landed("c9")
+        if last is not None:
+            last()
+        self.landed("a7")
+        self.landed("b7")
         keep.wait()
         for at, (name, direction, same, dz, half) in enumerate(self.MOVES):
             other = self.slot(self.block(*self.came(at), 1 - self.core), half)
@@ -516,6 +520,7 @@
 
             lax.fori_loop(0, 3 * width // block, one_block, 0)
 
+        def shorts_of(mb):
             def own_rows(at, carry):
                 columns = pl.ds(pl.multiple_of(at * block, block), block)
                 values = jnp.dot(
@@ -540,6 +545,7 @@
             relay(chunk).start()
 
         streams(0)
+        shorts_of(0)
         medium(0, 0, 64)
         reduce_start(fine[0])
         medium(0, 64, length - 64)
@@ -548,9 +554,10 @@
         streams(1)
         reduce_middle(fine[1])
         pass_on(0)
+        shorts_of(1)
+        pass_on(1)
         medium(1, 0, 80)
         reduce_start(fine[2])
-        pass_on(1)
         medium(1, 80, length - 80)
         reduce_middle(fine[2])
         reduce_start(fine[3])
@@ -740,10 +747,12 @@
             gather_middle(0)
             gather_start(1)
 
+        def later():
+            gather_middle(1)
+
         spread_weight = Gather(slot, shard, send, recv, side_send, side_recv)
-        spread_weight.run(local.at[0], early)
+        spread_weight.run(local.at[0], early, later)
         load_weight.wait()
-        gather_middle(1)
         gather_end(0)
         gather_end(1)
         project(0)

time: 164 us -> 164 us (level)
  no operation moved by 1% of the time
where the time goes in v7:
time: 164 us
  Pallas kernels  162 us (99%)
  local copies, waits for them, and re-layouts  1.9 us (1%)
    pallas_call x1, Pallas kernels, body(): pl.pallas_call(mixer_kernel, out_shape=jax.ShapeDtypeStruct((rows, width)...  162 us

profile of v7, /device:TPU:26, one launch (start us, length us, event | category | flops | bytes accessed | tf_op | source)
XLA Modules:
  0.0 163.7 jit_solution(14135470866877363148)
XLA Ops:
  0.0 161.8 %mixer.1 = bf16[288,1024]{1,0:T(8,128)(2,1)} custom-call(s32[2,136]{1,0:T(2,128)} %ids.1, bf16[3,128,1024]{2,1,0:T(8,128)(2,1)} %bitcast.9, bf16[512,1024]{1,0:T(8,128)(2,1)} %table.1, f32[1,4096]{1,0:T(1,128)} %gain.1, f32[3,7,1,1024]{3,2,1,0:T(1,128)} %bitcast.11, f32[128,1024]{1,0:T(8,128)} %bitcast.10, bf16[1024,4096]{1,0:T(8,128)(2,1)} %bitcast.7), custom_call_target="tpu_custom_call" | custom-call | tf_op jit(solution)/shard_map/mixer/pallas_call | solution.py:812
  161.8 1.9 %slice.4 = bf16[1,2,136,1024]{3,2,1,0:T(8,128)(2,1)} slice(bf16[1,2,144,1024]{3,2,1,0:T(8,128)(2,1)} %bitcast.8), slice={[0:1], [0:2], [0:136], [0:1024]} | slice | bytes 1114112 | tf_op jit(solution)/shard_map/slice | solution.py:861

commit v8 on v7

--- a/solution.py
+++ b/solution.py
@@ -634,7 +634,7 @@
                 share_out(chunk, 1, tensor, behind).wait_send()
                 share_out(chunk, 2, behind, ahead).wait_send()
 
-        def project(group):
+        def project(group, begin, end):
             first, rows = group * pitch, pitch
             lines = 16
 
@@ -652,7 +652,8 @@
                 base[window] = xs[tensor, window].astype(jnp.float32)
                 return carry
 
-            lax.fori_loop(0, rows // lines, normalise, 0)
+            if begin > 0:
+                lax.fori_loop(0, rows // lines, normalise, 0)
 
             def one_block(at, carry):
                 stream, inner = at // (width // block), at % (width // block)
@@ -671,7 +672,9 @@
                     sf[stream, tile, first + 8 : first + 8 + length, :] = piece[0:length]
                 return carry
 
-            lax.fori_loop(0, 3 * width // block, one_block, 0)
+            lax.fori_loop(begin, end, one_block, 0)
+
+        third = width // block
 
         def rim(mb):
             return remote(
@@ -709,6 +712,9 @@
             def _():
                 gated_rim(mb).start()
 
+        def shorts_end(mb):
+            first = mb * pitch
+
             @pl.when(seq > 0)
             def _():
                 rim(mb).wait_recv()
@@ -755,10 +761,12 @@
         load_weight.wait()
         gather_end(0)
         gather_end(1)
-        project(0)
+        project(0, third, 3 * third)
+        shorts(0)
+        project(0, 0, third)
         rim_start(0)
         gather_start(2)
-        shorts(0)
+        shorts_end(0)
         gather_middle(2)
         gather_start(3)
         spread_weight.close()
@@ -769,10 +777,12 @@
         reduce_start(coarse[0])
         gather_end(2)
         gather_end(3)
-        project(1)
+        project(1, third, 3 * third)
+        shorts(1)
+        project(1, 0, third)
         rim_start(1)
         reduce_middle(coarse[0])
-        shorts(1)
+        shorts_end(1)
         gated_end(1)
         medium(1, 0, 80)
         reduce_start(coarse[1])

time: 164 us -> 165 us (level)
  no operation moved by 1% of the time
where the time goes in v8:
time: 165 us; the launch traced here: 164 us
  Pallas kernels  163 us (99%)
  local copies, waits for them, and re-layouts  1.9 us (1%)
    pallas_call x1, Pallas kernels, body(): pl.pallas_call(mixer_kernel, out_shape=jax.ShapeDtypeStruct((rows, width)...  163 us

profile of v8, /device:TPU:26, one launch (start us, length us, event | category | flops | bytes accessed | tf_op | source)
XLA Modules:
  0.0 164.5 jit_solution(3939380298955791526)
XLA Ops:
  0.0 162.6 %mixer.1 = bf16[288,1024]{1,0:T(8,128)(2,1)} custom-call(s32[2,136]{1,0:T(2,128)} %ids.1, bf16[3,128,1024]{2,1,0:T(8,128)(2,1)} %bitcast.9, bf16[512,1024]{1,0:T(8,128)(2,1)} %table.1, f32[1,4096]{1,0:T(1,128)} %gain.1, f32[3,7,1,1024]{3,2,1,0:T(1,128)} %bitcast.11, f32[128,1024]{1,0:T(8,128)} %bitcast.10, bf16[1024,4096]{1,0:T(8,128)(2,1)} %bitcast.7), custom_call_target="tpu_custom_call" | custom-call | tf_op jit(solution)/shard_map/mixer/pallas_call | solution.py:822
  162.6 1.9 %slice.4 = bf16[1,2,136,1024]{3,2,1,0:T(8,128)(2,1)} slice(bf16[1,2,144,1024]{3,2,1,0:T(8,128)(2,1)} %bitcast.8), slice={[0:1], [0:2], [0:136], [0:1024]} | slice | bytes 1114112 | tf_op jit(solution)/shard_map/slice | solution.py:871
